TPU v7x, 256 devices: a whole 4x4x8 slice. The times are simulated.
256 devices in a mesh: ulysses: 8 (over y, x_hi), blk: 32 (over x_lo, z, core).
Axes of the slice: x: 4 (x_hi: 2, x_lo: 2; x = x_hi * 2 + x_lo), y: 4, z: 8, core: 2. Of those that a mesh axis runs over, the one named last changes fastest.
Arguments:
- image_tokens: bfloat16 [8192, 3072], P(('blk', 'ulysses')), may hold values from -110 to 110
- text_tokens: bfloat16 [256, 3072], P('blk'), may hold values from -6 to 6
- modulation: float32 [3, 3072], replicated, may hold values from -4 to 4
- text_modulation: float32 [2, 3072], replicated, may hold values from -4 to 4
- norm_gains: float32 [3, 128], replicated, may hold values from 0.5 to 9
- qkv_weight: bfloat16 [3072, 24, 384], P(None, 'ulysses'), may hold values from -0.07289047 to 0.07289047
- text_kv_weight: bfloat16 [3072, 24, 256], P('blk', 'ulysses'), may hold values from -0.109375 to 0.109375
- out_weight: bfloat16 [3072, 3072], P('ulysses'), may hold values from -0.109375 to 0.109375
Outputs:
- block_out: bfloat16 [8192, 3072], P(('blk', 'ulysses'))
All inputs are finite; a program needn't handle non-finite values.
Results may differ from a plain program's by a relative error of at most 0.015.
Values may be sent and summed in bfloat16 or wider, within the bound.
A program may use at most 128 MiB of HBM per device.

v0:
```python
import jax
import jax.numpy as jnp
from jax import lax
from jax.sharding import PartitionSpec as P


def modulate(token_rows, shift, scale):
    values = token_rows.astype(jnp.float32)
    average = jnp.mean(values, axis=-1, keepdims=True)
    spread = jnp.mean((values - average) ** 2, axis=-1, keepdims=True)
    normed = (values - average) * lax.rsqrt(spread + 1e-06)
    return (normed * (1.0 + scale) + shift).astype(jnp.bfloat16)


def root_normalize(values, gain):
    squares = jnp.mean(values * values, axis=-1, keepdims=True)
    return (values * lax.rsqrt(squares + 1e-06) * gain).astype(jnp.bfloat16)


def attend(state, queries, key_block, value_block):
    maximum, denominator, numerator = state
    scale_factor = queries.shape[-1] ** (-0.5)
    scores = (
        jnp.einsum("qhd,khd->qhk", queries, key_block, preferred_element_type=jnp.float32)
        * scale_factor
    )
    new_maximum = jnp.maximum(maximum, jnp.max(scores, axis=-1))
    expo = jnp.exp(scores - new_maximum[..., None])
    factor = jnp.exp(maximum - new_maximum)
    denominator = denominator * factor + jnp.sum(expo, axis=-1)
    update = jnp.einsum(
        "qhk,khd->qhd", expo.astype(jnp.bfloat16), value_block, preferred_element_type=jnp.float32
    )
    numerator = numerator * factor[..., None] + update
    return (new_maximum, denominator, numerator)


def attend_blocks(state, queries, key_rows, value_rows):
    total_rows = key_rows.shape[0]
    block_size = 1024
    block_count = total_rows // block_size
    if block_count == 0:
        return attend(state, queries, key_rows, value_rows)
    shaped_keys = key_rows.reshape((block_count, block_size) + key_rows.shape[1:])
    shaped_values = value_rows.reshape((block_count, block_size) + value_rows.shape[1:])

    def scan_step(carried, blocks):
        return (attend(carried, queries, blocks[0], blocks[1]), None)

    state, _ = lax.scan(scan_step, state, (shaped_keys, shaped_values))
    return state


def per_device(
    image_tokens,
    text_tokens,
    modulation,
    text_modulation,
    norm_gains,
    qkv_weight,
    text_kv_weight,
    out_weight,
):
    heads_here = qkv_weight.shape[1]
    head_size = qkv_weight.shape[2] // 3
    modulated = modulate(image_tokens, modulation[0], modulation[1])
    gathered = lax.all_gather(modulated, "ulysses", axis=0, tiled=True)
    query_count = gathered.shape[0]
    caption_local = modulate(text_tokens, text_modulation[0], text_modulation[1])
    caption_source = lax.all_gather(caption_local, "blk", axis=0, tiled=True)
    piece = lax.all_gather(text_kv_weight, "blk", axis=0, tiled=True)
    piece_rows = piece.shape[0]
    caption_projected = jnp.dot(
        caption_source, piece.reshape(piece_rows, -1), preferred_element_type=jnp.float32
    )
    projected = jnp.dot(
        gathered, qkv_weight.reshape(qkv_weight.shape[0], -1), preferred_element_type=jnp.float32
    )
    projected = projected.reshape(query_count, heads_here, 3, head_size)
    queries = root_normalize(projected[:, :, 0], norm_gains[0])
    image_keys = root_normalize(projected[:, :, 1], norm_gains[1])
    image_values = projected[:, :, 2].astype(jnp.bfloat16)
    caption_projected = caption_projected.reshape(-1, heads_here, 2, head_size)
    caption_keys = root_normalize(caption_projected[:, :, 0], norm_gains[2])
    caption_values = caption_projected[:, :, 1].astype(jnp.bfloat16)
    empty_state = (
        jnp.full((query_count, heads_here), -1e30, jnp.float32),
        jnp.zeros((query_count, heads_here), jnp.float32),
        jnp.zeros((query_count, heads_here, head_size), jnp.float32),
    )
    first_state = attend_blocks(empty_state, queries, caption_keys, caption_values)
    maximum, denominator, numerator = attend_blocks(
        first_state,
        queries,
        lax.all_gather(image_keys, "blk", axis=0, tiled=True),
        lax.all_gather(image_values, "blk", axis=0, tiled=True),
    )
    attention = (
        (numerator / denominator[..., None])
        .astype(jnp.bfloat16)
        .reshape(query_count, heads_here * head_size)
    )
    projection = lax.psum_scatter(
        jnp.dot(attention, out_weight, preferred_element_type=jnp.float32).astype(jnp.bfloat16),
        "ulysses",
        scatter_dimension=0,
        tiled=True,
    ).astype(jnp.float32)
    return (image_tokens.astype(jnp.float32) + modulation[2] * projection).astype(jnp.bfloat16)


def solution(mesh):
    in_specs = (
        P(("blk", "ulysses"), None),
        P("blk", None),
        P(),
        P(),
        P(),
        P(None, "ulysses", None),
        P("blk", "ulysses", None),
        P("ulysses", None),
    )
    out_specs = P(("blk", "ulysses"), None)
    return jax.shard_map(
        per_device, mesh=mesh, in_specs=in_specs, out_specs=out_specs, check_vma=False
    )
```

profile of v0, /device:TPU:1, one launch (start us, length us, event | category | flops | bytes accessed | tf_op | source)
XLA Modules:
  0.0 503.2 jit_solution(4601074306459319905)
XLA Ops:
  6.5 1.0 fusion.49
  7.6 1.1 convert_reduce_fusion
  8.6 1.2 fusion.31
  9.8 1.8 fusion.34
  11.6 0.7 all-gather.9.cloned.1.call-update
  12.4 0.9 convert_reduce_fusion.1
  13.3 1.0 fusion.44
  14.3 0.8 slice_add_fusion.1
  15.2 1.5 fusion.47
  16.8 10.3 %copy.27 = bf16[3072,3,384]{0,2,1:T(8,128)(2,1)} copy(bf16[3072,3,384]{2,0,1:T(8,128)(2,1)} %param.15) | data formatting | bytes 14155776 | tf_op args[5]
  27.1 0.6 slice_bitcast_fusion.3
  27.7 42.0 %all-gather.11.cloned.1.call-done = bf16[256,3072]{1,0:T(8,128)(2,1)} async-done(((bf16[32,3072]{1,0:T(8,128)(2,1)}), bf16[256,3072]{1,0:T(8,128)(2,1)}) %all-gather.11.cloned.1.call-update) | async-done | bytes 1572880 | tf_op jit(solution)/shard_map/all_gather | solution.py:67
  69.7 5.5 %fusion.21 = f32[256,3,3,128]{0,3,2,1:T(8,128)S(1)} fusion(bf16[3,3,128,3072]{3,2,1,0:T(8,128)(2,1)} %bitcast.123, bf16[256,3072]{1,0:T(8,128)(2,1)} %all-gather.11.cloned.1.call-done), kind=kOutput, calls=%fused_computation.21 | convolution fusion | flops 1811939328 | bytes 9830400 | tf_op jit(solution)/shard_map/dot_general | solution.py:76
  75.3 0.9 multiply_convert_fusion
  76.3 0.7 slice.85
  77.2 1.1 copy.32
  78.3 60.7 %all-gather.9.cloned.1.call-done = bf16[3072,3,256]{2,0,1:T(8,128)(2,1)} async-done(((bf16[96,3,256]{2,0,1:T(8,128)(2,1)}), bf16[3072,3,256]{2,0,1:T(8,128)(2,1)}) %all-gather.9.cloned.1.call-update) | async-done | bytes 4718608 | tf_op jit(solution)/shard_map/all_gather | solution.py:71
  139.0 6.7 %copy.26 = bf16[3072,3,256]{0,2,1:T(8,128)(2,1)} copy(bf16[3072,3,256]{2,0,1:T(8,128)(2,1)} %all-gather.9.cloned.1.call-done) | data formatting | bytes 9437184 | tf_op jit(solution)/shard_map/all_gather | solution.py:71
  145.7 59.3 %all-gather.7.cloned.1.call-done = bf16[256,3072]{1,0:T(8,128)(2,1)} async-done(((bf16[8,3072]{1,0:T(8,128)(2,1)}), bf16[256,3072]{1,0:T(8,128)(2,1)}) %all-gather.7.cloned.1.call-update) | async-done | bytes 1572880 | tf_op jit(solution)/shard_map/all_gather | solution.py:70
  204.9 4.3 fusion.23
  210.1 76.7 %all-gather.13.cloned.1.call-done = bf16[8192,3,128]{0,2,1:T(8,128)(2,1)} async-done(((bf16[256,3,128]{0,2,1:T(8,128)(2,1)}), bf16[8192,3,128]{0,2,1:T(8,128)(2,1)}) %all-gather.13.cloned.1.call-update) | async-done | bytes 6291472 | tf_op jit(solution)/shard_map/all_gather | solution.py:95
  286.8 12.7 %copy.40 = bf16[48,8,8,1024]{3,2,1,0:T(8,128)(2,1)} copy(bf16[48,8,8,1024]{3,1,2,0:T(8,128)(2,1)} %bitcast.124) | data formatting | bytes 12582912
  299.4 9.2 %copy.31 = bf16[8,1024,3,128]{3,1,2,0:T(8,128)(2,1)} copy(bf16[8,1024,3,128]{1,0,3,2:T(8,128)(2,1)} %bitcast.121) | data formatting | bytes 12582912 | tf_op jit(solution)/shard_map/while | solution.py:50
  308.6 58.5 %all-gather.15.cloned.1.call-done = bf16[8192,3,1,128]{0,3,2,1:T(8,128)(2,1)} async-done(((bf16[256,3,1,128]{0,3,2,1:T(8,128)(2,1)}), bf16[8192,3,1,128]{0,3,2,1:T(8,128)(2,1)}) %all-gather.15.cloned.1.call-update) | async-done | bytes 6291472 | tf_op jit(solution)/shard_map/all_gather | solution.py:96
  367.1 10.0 %copy.41 = bf16[48,8,8,1024]{3,2,1,0:T(8,128)(2,1)S(1)} copy(bf16[48,8,8,1024]{3,1,2,0:T(8,128)(2,1)} %bitcast.125) | data formatting | bytes 12582912
  377.2 6.2 %copy.33 = bf16[8,1024,3,128]{1,3,2,0:T(8,128)(2,1)} copy(bf16[8,1024,3,128]{1,0,3,2:T(8,128)(2,1)S(1)} %bitcast.122) | data formatting | bytes 12582912 | tf_op jit(solution)/shard_map/while | solution.py:50
  383.4 33.7 %while.14 = (s32[]{:T(128)}, f32[256,3]{0,1:T(4,128)S(1)}, f32[256,3]{0,1:T(4,128)S(1)}, f32[256,3,128]{0,2,1:T(8,128)S(1)}, bf16[8,1024,3,128]{3,1,2,0:T(8,128)...) while((s32[]{:T(128)}, f32[256,3]{0,1:T(4,128)S(1)}, ...), condition=%wide.region_12.13_spmd, body=%wide.region_9.12_spmd.sunk | while | flops 409142784 | bytes 12043349 | solution.py:50
  383.4 1.7 bitcast_reduce_fusion.2
  385.1 0.5 fusion.65
  385.7 1.9 fusion.66
  387.6 1.7 bitcast_reduce_fusion.2
  389.3 0.5 fusion.65
  389.9 1.9 fusion.66
  391.8 1.7 bitcast_reduce_fusion.2
  394.1 1.9 fusion.66
  396.1 1.7 bitcast_reduce_fusion.2
  398.3 1.9 fusion.66
  400.3 1.7 bitcast_reduce_fusion.2
  402.6 1.9 fusion.66
  404.5 1.7 bitcast_reduce_fusion.2
  406.8 1.9 fusion.66
  408.7 1.7 bitcast_reduce_fusion.2
  411.0 1.9 fusion.66
  412.9 1.7 bitcast_reduce_fusion.2
  415.2 1.9 fusion.66
  417.2 2.2 convolution_convert_fusion
  419.4 75.3 %reduce-scatter.2.cloned.1.call-done = bf16[32,3072]{1,0:T(8,128)(2,1)} async-done(((bf16[256,3072]{1,0:T(8,128)(2,1)}), bf16[32,3072]{1,0:T(8,128)(2,1)}) %reduce-scatter.2.cloned.1.call-update) | async-done | bytes 196624 | tf_op jit(solution)/shard_map/reduce_scatter | solution.py:103
  494.7 1.7 fusion.35
  (67 shorter events, 4.9 us)
Async XLA Ops:
  6.5 410.7 %copy-start = (bf16[384,3072]{1,0:T(8,128)(2,1)S(1)}, bf16[384,3072]{1,0:T(8,128)(2,1)}, u32[]{:S(2)}) copy-start(bf16[384,3072]{1,0:T(8,128)(2,1)} %param.17) | copy-start | bytes 7077892
  6.5 63.1 %all-gather.11.cloned.1.call-start = ((), (), s32[]{:S(2)}) async-start(), calls=%async_computation.3 | async-start | bytes 1769472 | tf_op jit(solution)/shard_map/all_gather | solution.py:67
  11.6 127.4 %all-gather.9.cloned.1.call-start = ((), (), s32[]{:S(2)}) async-start(), calls=%async_computation.2 | async-start | bytes 4866048 | tf_op jit(solution)/shard_map/all_gather | solution.py:71
  12.3 192.6 %all-gather.7.cloned.1.call-start = ((), (), s32[]{:S(2)}) async-start(), calls=%async_computation.1 | async-start | bytes 1622016 | tf_op jit(solution)/shard_map/all_gather | solution.py:70
  16.7 10.3 %copy-start.5 = (f32[3,128]{1,0:T(4,128)S(1)}, f32[3,128]{1,0:T(4,128)}, u32[]{:S(2)}) copy-start(f32[3,128]{1,0:T(4,128)} %param.14) | copy-start | bytes 4612
  16.7 270.1 %all-gather.13.cloned.1.call-start = ((), (), s32[]{:S(2)}) async-start(), calls=%async_computation.4 | async-start | bytes 6488064 | tf_op jit(solution)/shard_map/all_gather | solution.py:95
  69.7 5.6 %copy-start.3 = (f32[128]{0:T(128)S(1)}, f32[128]{0:T(128)}, u32[]{:S(2)}) copy-start(f32[128]{0:T(128)} %get-tuple-element.95) | copy-start | bytes 1540
  69.7 5.7 %copy-start.4 = (f32[128]{0:T(128)S(1)}, f32[128]{0:T(128)}, u32[]{:S(2)}) copy-start(f32[128]{0:T(128)} %get-tuple-element.97) | copy-start | bytes 1540
  76.2 290.9 %all-gather.15.cloned.1.call-start = ((), (), s32[]{:S(2)}) async-start(), calls=%async_computation.6 | async-start | bytes 6488064 | tf_op jit(solution)/shard_map/all_gather | solution.py:96
  77.0 417.7 %reduce-scatter.2.cloned.1.call-start = ((), (), s32[]{:S(2)}) async-start(), calls=%async_computation.5 | async-start | bytes 1769472 | tf_op jit(solution)/shard_map/reduce_scatter | solution.py:103
  204.9 4.3 copy-start.2
  417.1 77.6 %copy-start.1 = (bf16[32,3072]{1,0:T(8,128)(2,1)S(1)}, bf16[32,3072]{1,0:T(8,128)(2,1)}, u32[]{:S(2)}) copy-start(bf16[32,3072]{1,0:T(8,128)(2,1)} %param.10) | copy-start | bytes 589828
Sparse Core Ops, SparseCore 0:
  11.7 57.9 all-gather.10
  71.5 67.4 all-gather.8
  140.9 64.0 all-gather.6
  206.5 80.1 all-gather.12
  288.4 78.7 all-gather.14
  419.5 75.1 reduce-scatter.1
where the time goes:
time: 505 us; the launch traced here: 503 us
  waiting for transfers between devices  373 us (74%)
  local copies, waits for them, and re-layouts  57.4 us (11%)
  matrix products  41.6 us (8%)
  other arithmetic  16.6 us (3%)
  between operations  13.6 us (3%)
    all_gather x1, waiting for transfers between devices, per_device(): lax.all_gather(image_keys, 'blk', axis=0, tiled=True)  76.7 us
    reduce_scatter x1, waiting for transfers between devices, per_device(): lax.psum_scatter(jnp.dot(attention, out_weight, preferred_element_type=jn...  75.3 us
    all_gather x1, waiting for transfers between devices, per_device(): piece = lax.all_gather(text_kv_weight, 'blk', axis=0, tiled=True)  60.7 us
    all_gather x1, waiting for transfers between devices, per_device(): caption_source = lax.all_gather(caption_local, 'blk', axis=0, tiled=True)  59.3 us
    all_gather x1, waiting for transfers between devices, per_device(): lax.all_gather(image_values, 'blk', axis=0, tiled=True)  58.5 us
    all_gather x1, waiting for transfers between devices, per_device(): gathered = lax.all_gather(modulated, 'ulysses', axis=0, tiled=True)  42 us
    unnamed x15, local copies, waits for them, and re-layouts  33 us
    while x3, local copies, waits for them, and re-layouts, attend_blocks(): state, _ = lax.scan(scan_step, state, (shaped_keys, shaped_values))  16.5 us
  transfers between devices with their start and end apart: 6, of which 6 were waited for; matrix products, arithmetic and copies ran while one was open for 11% of the time, Pallas kernels for 0%

commit v1 on v0

v1 whole, which is shorter than its diff:
```python
import math

import jax
import jax.numpy as jnp
from jax import lax
from jax.experimental import pallas as pl
from jax.experimental.pallas import tpu as pltpu
from jax.sharding import PartitionSpec as P

D = 3072
HEAD = 128
HEADS_HERE = 3
ROWS = 32
BLOCK = 256
CAP_COLS = 96
CAP_ROWS = 8
CHUNKS = 4
CHUNK = D // CHUNKS
MESH = pl.DeviceIdType.MESH
F32 = jnp.float32
BF16 = jnp.bfloat16
QUERY_SCALE = math.log2(math.e) / math.sqrt(HEAD)
LOG2E = math.log2(math.e)
ULYSSES_STEPS = [(1, 0), (3, 0), (2, 0), (0, 1), (1, 1), (3, 1), (2, 1)]


def layer_norm(values, shift, scale):
    average = jnp.mean(values, axis=-1, keepdims=True)
    centered = values - average
    spread = jnp.mean(centered * centered, axis=-1, keepdims=True)
    return (centered * lax.rsqrt(spread + 1e-06) * (1.0 + scale) + shift).astype(BF16)


def root_norm(values, gain):
    squares = jnp.mean(values * values, axis=-1, keepdims=True)
    return (values * lax.rsqrt(squares + 1e-06) * gain).astype(BF16)


def kernel(
    img_ref, text_ref, mod_ref, tmod_ref, gains_ref, qkv_hbm, tkv_hbm, out_hbm,
    out_ref,
    w_qkv, w_cap, w_out, tok, cap_send, cap_recv, part, part_recv, cap_all,
    q_buf, kv, m_buf, acc, o_send, o_recv, l_send, l_recv, att, p_send, p_recv, p_own,
    w_sem, tok_send, tok_recv, cap_sems, part_sems, capall_sems,
    q_send, q_recv, right_send, right_recv, left_send, left_recv,
    o_ssem, o_rsem, l_ssem, l_rsem, p_ssem, p_rsem,
):
    u = lax.axis_index("ulysses")
    b = lax.axis_index("blk")
    y, xh = u // 2, lax.rem(u, 2)
    xl, z, c = b // 16, lax.rem(b // 2, 8), lax.rem(b, 2)

    def ulysses_peer(dy, dx):
        return lax.rem(y + dy, 4) * 2 + lax.rem(xh + dx, 2)

    def blk_of(xl_, z_, c_):
        return xl_ * 16 + z_ * 2 + c_

    load_cap = pltpu.make_async_copy(tkv_hbm, w_cap.at[:, pl.ds(0, CAP_COLS), :], w_sem.at[0])
    load_qkv = pltpu.make_async_copy(qkv_hbm, w_qkv, w_sem.at[1])
    load_out = pltpu.make_async_copy(out_hbm, w_out, w_sem.at[2])
    load_cap.start()
    load_qkv.start()
    load_out.start()

    barrier = pltpu.get_barrier_semaphore()
    for dy, dx in ULYSSES_STEPS:
        pl.semaphore_signal(
            barrier, inc=1, device_id={"ulysses": ulysses_peer(dy, dx)}, device_id_type=MESH
        )

    def greet(r, carry):
        pl.semaphore_signal(
            barrier, inc=1, device_id={"blk": lax.rem(b + r, 32)}, device_id_type=MESH
        )
        return carry

    lax.fori_loop(1, 32, greet, 0)

    tok[0] = layer_norm(img_ref[...].astype(F32), mod_ref[0:1, :], mod_ref[1:2, :])

    cap = layer_norm(text_ref[...].astype(F32), tmod_ref[0:1, :], tmod_ref[1:2, :]).astype(F32)
    groups = jnp.concatenate([cap[:, 384 * g : 384 * g + 384] for g in range(8)], axis=0)
    row = lax.broadcasted_iota(jnp.int32, (384, 512), 0)
    col = lax.broadcasted_iota(jnp.int32, (384, 512), 1)
    lane = lax.rem(col, 128)
    pick = jnp.where((lane < CAP_COLS) & (row == (col // 128) * CAP_COLS + lane), 1.0, 0.0)
    pieces = jnp.dot(groups.astype(BF16), pick.astype(BF16), preferred_element_type=F32)
    for g in range(8):
        for t in range(4):
            cap_send[4 * g + t] = pieces[8 * g : 8 * g + 8, 128 * t : 128 * t + 128]
    for h in range(HEADS_HERE):
        w_cap[h, CAP_COLS:128, :] = jnp.zeros((128 - CAP_COLS, 256), BF16)

    pl.semaphore_wait(barrier, 38)

    def send_caption(r, carry):
        to = lax.rem(b + r, 32)
        pltpu.make_async_remote_copy(
            src_ref=cap_send.at[to], dst_ref=cap_recv.at[b],
            send_sem=cap_sems.at[0], recv_sem=cap_sems.at[1],
            device_id={"blk": to}, device_id_type=MESH,
        ).start()
        return carry

    lax.fori_loop(1, 32, send_caption, 0)

    def token_copy(i):
        dy, dx = ULYSSES_STEPS[i]
        return pltpu.make_async_remote_copy(
            src_ref=tok.at[0], dst_ref=tok.at[i + 1],
            send_sem=tok_send.at[i], recv_sem=tok_recv.at[i],
            device_id={"ulysses": ulysses_peer(dy, dx)}, device_id_type=MESH,
        )

    for i in range(7):
        token_copy(i).start()

    cap_recv[b] = cap_send[b]
    load_cap.wait()
    cap_done = pltpu.make_async_remote_copy(
        src_ref=cap_send.at[pl.ds(0, 31)], dst_ref=cap_recv.at[pl.ds(0, 31)],
        send_sem=cap_sems.at[0], recv_sem=cap_sems.at[1],
        device_id={"blk": lax.rem(b + 1, 32)}, device_id_type=MESH,
    )
    cap_done.wait_recv()
    cap_rows = cap_recv[...].reshape(256, 128).astype(BF16)
    for h in range(HEADS_HERE):
        product = jnp.dot(cap_rows, w_cap[h], preferred_element_type=F32)
        both = jnp.concatenate(
            [product[:, :128].reshape(32, 8, 128), product[:, 128:].reshape(32, 8, 128)], axis=1
        )
        part[:, :, h * 128 : (h + 1) * 128] = both.astype(BF16)

    def send_part(r, carry):
        to = lax.rem(b + r, 32)
        pltpu.make_async_remote_copy(
            src_ref=part.at[to], dst_ref=part_recv.at[b],
            send_sem=part_sems.at[0], recv_sem=part_sems.at[1],
            device_id={"blk": to}, device_id_type=MESH,
        ).start()
        return carry

    lax.fori_loop(1, 32, send_part, 0)
    part_recv[b] = part[b]
    part_done = pltpu.make_async_remote_copy(
        src_ref=part.at[pl.ds(0, 31)], dst_ref=part_recv.at[pl.ds(0, 31)],
        send_sem=part_sems.at[0], recv_sem=part_sems.at[1],
        device_id={"blk": lax.rem(b + 1, 32)}, device_id_type=MESH,
    )
    part_done.wait_recv()
    total = jnp.sum(part_recv[...].astype(F32), axis=0)
    for h in range(HEADS_HERE):
        cols = slice(h * 128, (h + 1) * 128)
        key_rows = root_norm(total[0:8, cols], gains_ref[2:3, :]).astype(F32)
        cap_all[0, :, cols] = jnp.concatenate([key_rows, total[8:16, cols]], axis=0).astype(BF16)

    def capall_copy(dz):
        return pltpu.make_async_remote_copy(
            src_ref=cap_all.at[0], dst_ref=cap_all.at[dz],
            send_sem=capall_sems.at[0, dz], recv_sem=capall_sems.at[1, dz],
            device_id={"blk": blk_of(xl, lax.rem(z + dz, 8), c)}, device_id_type=MESH,
        )

    for dz in range(1, 8):
        capall_copy(dz).start()

    right_peer = {"blk": blk_of(xl, lax.rem(z + 1, 8), c)}
    left_peer = {"blk": blk_of(xl, lax.rem(z + 7, 8), c)}

    def ring_right(h, s):
        src, dst = kv.at[h, s - 1], kv.at[h, s]
        if s == 4:
            src, dst = src.at[0], dst.at[0]
        return pltpu.make_async_remote_copy(
            src_ref=src, dst_ref=dst, send_sem=right_send.at[h, s - 1],
            recv_sem=right_recv.at[h, s - 1], device_id=right_peer, device_id_type=MESH,
        )

    def ring_left(h, s):
        src, dst = kv.at[h, (9 - s) % 8], kv.at[h, 8 - s]
        if s == 4:
            src, dst = src.at[1], dst.at[1]
        return pltpu.make_async_remote_copy(
            src_ref=src, dst_ref=dst, send_sem=left_send.at[h, s - 1],
            recv_sem=left_recv.at[h, s - 1], device_id=left_peer, device_id_type=MESH,
        )

    def quad_peer(j):
        return {"blk": blk_of(lax.rem(xl + j // 2, 2), z, lax.rem(c + j % 2, 2))}

    def query_copy(h, j):
        return pltpu.make_async_remote_copy(
            src_ref=q_buf.at[h, 0], dst_ref=q_buf.at[h, j],
            send_sem=q_send.at[h, j], recv_sem=q_recv.at[h, j],
            device_id=quad_peer(j), device_id_type=MESH,
        )

    load_qkv.wait()
    for i in range(7):
        token_copy(i).wait_recv()

    def project(h, carry):
        rows = tok[...].reshape(BLOCK, D)
        projected = jnp.dot(rows, w_qkv[h], preferred_element_type=F32)
        kv[h, 0, 0] = root_norm(projected[:, 128:256], gains_ref[1:2, :])
        kv[h, 0, 1] = projected[:, 256:384].astype(BF16)
        ring_right(h, 1).start()
        ring_left(h, 1).start()
        q_buf[h, 0] = root_norm(projected[:, 0:128], gains_ref[0:1, :] * QUERY_SCALE)
        for j in range(1, 4):
            query_copy(h, j).start()
        return carry

    lax.fori_loop(0, HEADS_HERE, project, 0)

    ones = jnp.ones((BLOCK, 128), BF16)

    def attend(h, slots, first=False, caption=None):
        def tile(t, carry):
            q = q_buf[h, t]
            keys = [kv[h, s, 0] for s in slots]
            values = [kv[h, s, 1] for s in slots]
            fill = [ones for _ in slots]
            if caption is not None:
                keys.append(caption[0])
                values.append(caption[1])
                fill.append(jnp.ones((64, 128), BF16))
            scores = [
                lax.dot_general(q, k, (((1,), (1,)), ((), ())), preferred_element_type=F32)
                for k in keys
            ]
            top = jnp.max(scores[0], axis=-1, keepdims=True)
            for s in scores[1:]:
                top = jnp.maximum(top, jnp.max(s, axis=-1, keepdims=True))
            if first:
                m_new = jnp.broadcast_to(top, (BLOCK, 128))
            else:
                m_old = m_buf[h, t]
                m_new = jnp.maximum(m_old, top)
            wide = jnp.concatenate([m_new, m_new], axis=1)
            update = None
            for s, v, o in zip(scores, values, fill):
                sub = wide if s.shape[1] == 256 else m_new[:, : s.shape[1]]
                weights = jnp.exp2(s - sub).astype(BF16)
                term = jnp.dot(
                    weights, jnp.concatenate([v, o], axis=1), preferred_element_type=F32
                )
                update = term if update is None else update + term
            if first:
                acc[h, t] = update
            else:
                alpha = jnp.exp2(m_old - m_new)
                acc[h, t] = acc[h, t] * jnp.concatenate([alpha, alpha], axis=1) + update
            m_buf[h, t] = m_new
            return carry

        lax.fori_loop(0, 4, tile, 0)

    def forward(h, s):
        ring_right(h, s - 1).wait_recv()
        ring_right(h, s).start()
        ring_left(h, s - 1).wait_recv()
        ring_left(h, s).start()

    def step_two(h, carry):
        forward(h, 2)
        return carry

    lax.fori_loop(0, HEADS_HERE, step_two, 0)

    for dz in range(1, 8):
        capall_copy(dz).wait_recv()

    def step_three(h, carry):
        forward(h, 3)
        for j in range(1, 4):
            query_copy(h, j).wait_recv()
        col = pl.ds(pl.multiple_of(h * 128, 128), 128)
        cap_kv = cap_all[:, :, col].astype(F32)
        cap_keys = cap_kv[:, 0:8, :].reshape(64, 128).astype(BF16)
        cap_values = cap_kv[:, 8:16, :].reshape(64, 128).astype(BF16)
        attend(h, [0], first=True, caption=(cap_keys, cap_values))
        attend(h, [1, 7])
        return carry

    lax.fori_loop(0, HEADS_HERE, step_three, 0)

    def step_four(h, carry):
        forward(h, 4)
        attend(h, [2, 6])
        attend(h, [3, 5])
        return carry

    lax.fori_loop(0, HEADS_HERE, step_four, 0)

    def o_copy(h, j):
        return pltpu.make_async_remote_copy(
            src_ref=o_send.at[h, j], dst_ref=o_recv.at[h, j],
            send_sem=o_ssem.at[h, j], recv_sem=o_rsem.at[h, j],
            device_id=quad_peer(j), device_id_type=MESH,
        )

    def l_copy(h, j):
        return pltpu.make_async_remote_copy(
            src_ref=l_send.at[h, j], dst_ref=l_recv.at[h, j],
            send_sem=l_ssem.at[h, j], recv_sem=l_rsem.at[h, j],
            device_id=quad_peer(j), device_id_type=MESH,
        )

    def step_last(h, carry):
        ring_right(h, 4).wait_recv()
        ring_left(h, 4).wait_recv()
        attend(h, [4])
        for j in range(1, 4):
            denominator = acc[h, j, :, 128:]
            o_send[h, j] = (acc[h, j, :, :128] / denominator).astype(BF16)
            level = m_buf[h, j] + jnp.log(denominator) * LOG2E
            l_send[h, j] = level.T[0:8, :]
            o_copy(h, j).start()
            l_copy(h, j).start()
        return carry

    lax.fori_loop(0, HEADS_HERE, step_last, 0)

    def combine(h, carry):
        denominator = acc[h, 0, :, 128:]
        outs = [acc[h, 0, :, :128] / denominator]
        levels = [m_buf[h, 0] + jnp.log(denominator) * LOG2E]
        for j in range(1, 4):
            o_copy(h, j).wait_recv()
            l_copy(h, j).wait_recv()
            outs.append(o_recv[h, j].astype(F32))
            levels.append(jnp.broadcast_to(l_recv[h, j][0:1, :], (128, BLOCK)).T)
        top = levels[0]
        for level in levels[1:]:
            top = jnp.maximum(top, level)
        numerator, weight = None, None
        for out, level in zip(outs, levels):
            share = jnp.exp2(level - top)
            numerator = out * share if numerator is None else numerator + out * share
            weight = share if weight is None else weight + share
        att[h] = (numerator / weight).astype(BF16)
        return carry

    lax.fori_loop(0, HEADS_HERE, combine, 0)

    load_out.wait()

    def p_copy(n, i):
        dy, dx = ULYSSES_STEPS[i]
        return pltpu.make_async_remote_copy(
            src_ref=p_send.at[n, i], dst_ref=p_recv.at[n, i],
            send_sem=p_ssem.at[n, i], recv_sem=p_rsem.at[n, i],
            device_id={"ulysses": ulysses_peer(4 - dy, 2 - dx)}, device_id_type=MESH,
        )

    def out_chunk(n, carry):
        cols = pl.ds(pl.multiple_of(n * CHUNK, 128), CHUNK)
        rows = jnp.concatenate([att[h] for h in range(HEADS_HERE)], axis=1)
        product = jnp.dot(rows, w_out[:, cols], preferred_element_type=F32)
        p_own[n] = product[0:ROWS]
        p_send[n] = product[ROWS:].astype(BF16).reshape(7, ROWS, CHUNK)
        for i in range(7):
            p_copy(n, i).start()
        return carry

    lax.fori_loop(0, CHUNKS, out_chunk, 0)

    def finish(n, carry):
        cols = pl.ds(pl.multiple_of(n * CHUNK, 128), CHUNK)
        for i in range(7):
            p_copy(n, i).wait_recv()
        projection = p_own[n] + jnp.sum(p_recv[n].astype(F32), axis=0)
        out_ref[:, cols] = (
            img_ref[:, cols].astype(F32) + mod_ref[2:3, cols] * projection
        ).astype(BF16)
        return carry

    lax.fori_loop(0, CHUNKS, finish, 0)

    cap_done.wait_send()
    part_done.wait_send()
    for i in range(7):
        token_copy(i).wait_send()
    for dz in range(1, 8):
        capall_copy(dz).wait_send()

    def drain_head(h, carry):
        for s in range(1, 5):
            ring_right(h, s).wait_send()
            ring_left(h, s).wait_send()
        for j in range(1, 4):
            query_copy(h, j).wait_send()
            o_copy(h, j).wait_send()
            l_copy(h, j).wait_send()
        return carry

    lax.fori_loop(0, HEADS_HERE, drain_head, 0)

    def drain_chunk(n, carry):
        for i in range(7):
            p_copy(n, i).wait_send()
        return carry

    lax.fori_loop(0, CHUNKS, drain_chunk, 0)


def per_device(
    image_tokens, text_tokens, modulation, text_modulation, norm_gains,
    qkv_weight, text_kv_weight, out_weight,
):
    qkv = jnp.transpose(qkv_weight, (1, 0, 2))
    tkv = jnp.transpose(text_kv_weight, (1, 0, 2))
    dma = pltpu.SemaphoreType.DMA
    vmem = pl.BlockSpec(memory_space=pltpu.VMEM)
    hbm = pl.BlockSpec(memory_space=pl.ANY)
    h3 = HEADS_HERE
    return pl.pallas_call(
        kernel,
        out_shape=jax.ShapeDtypeStruct((ROWS, D), BF16),
        in_specs=[vmem] * 5 + [hbm] * 3,
        out_specs=vmem,
        scratch_shapes=[
            pltpu.VMEM((h3, D, 384), BF16),
            pltpu.VMEM((h3, 128, 256), BF16),
            pltpu.VMEM((384, D), BF16),
            pltpu.VMEM((8, ROWS, D), BF16),
            pltpu.VMEM((32, 8, 128), F32),
            pltpu.VMEM((32, 8, 128), F32),
            pltpu.VMEM((32, 16, 384), BF16),
            pltpu.VMEM((32, 16, 384), BF16),
            pltpu.VMEM((8, 16, 384), BF16),
            pltpu.VMEM((h3, 4, BLOCK, 128), BF16),
            pltpu.VMEM((h3, 8, 2, BLOCK, 128), BF16),
            pltpu.VMEM((h3, 4, BLOCK, 128), F32),
            pltpu.VMEM((h3, 4, BLOCK, 256), F32),
            pltpu.VMEM((h3, 4, BLOCK, 128), BF16),
            pltpu.VMEM((h3, 4, BLOCK, 128), BF16),
            pltpu.VMEM((h3, 4, 8, BLOCK), F32),
            pltpu.VMEM((h3, 4, 8, BLOCK), F32),
            pltpu.VMEM((h3, BLOCK, 128), BF16),
            pltpu.VMEM((CHUNKS, 7, ROWS, CHUNK), BF16),
            pltpu.VMEM((CHUNKS, 7, ROWS, CHUNK), BF16),
            pltpu.VMEM((CHUNKS, ROWS, CHUNK), F32),
            dma((3,)), dma((7,)), dma((7,)), dma((2,)), dma((2,)), dma((2, 8)),
            dma((h3, 4)), dma((h3, 4)),
            dma((h3, 4)), dma((h3, 4)), dma((h3, 4)), dma((h3, 4)),
            dma((h3, 4)), dma((h3, 4)), dma((h3, 4)), dma((h3, 4)),
            dma((CHUNKS, 7)), dma((CHUNKS, 7)),
        ],
        compiler_params=pltpu.CompilerParams(
            collective_id=0, has_side_effects=True, vmem_limit_bytes=50 * 1024 * 1024
        ),
        name="joint_attention",
    )(image_tokens, text_tokens, modulation, text_modulation, norm_gains, qkv, tkv, out_weight)


def solution(mesh):
    in_specs = (
        P(("blk", "ulysses"), None),
        P("blk", None),
        P(),
        P(),
        P(),
        P(None, "ulysses", None),
        P("blk", "ulysses", None),
        P("ulysses", None),
    )
    out_specs = P(("blk", "ulysses"), None)
    return jax.shard_map(
        per_device, mesh=mesh, in_specs=in_specs, out_specs=out_specs, check_vma=False
    )
```

time: 505 us -> 122 us (0.24)
  waiting for transfers between devices: 373 us -> 0 us
  Pallas kernels: 0 us -> 115 us
  local copies, waits for them, and re-layouts: 57.4 us -> 7.19 us
  matrix products: 41.6 us -> 0 us
  other arithmetic: 16.6 us -> 0 us
  between operations: 13.6 us -> 0.02 us
    all_gather x5 -> x0, waiting for transfers between devices: 297 us -> none  [the longest x1 76.7 us: per_device(): lax.all_gather(image_keys, 'blk', axis=0, tiled=True)]
    pallas_call x0 -> x1, Pallas kernels: none -> 115 us  [per_device(): pl.pallas_call(kernel, out_shape=jax.ShapeDtypeStruct((ROWS, D), BF16), i...]
    reduce_scatter x1 -> x0, waiting for transfers between devices: 75.3 us -> none  [per_device(): lax.psum_scatter(jnp.dot(attention, out_weight, preferred_element_type=jn...]
    dot_general x21 -> x0, matrix products: 41.6 us -> none  [the longest x9 15.5 us: attend(): jnp.einsum('qhk,khd->qhd', expo.astype(jnp.bfloat16), value_block, prefer...]
    unnamed x15, local copies, waits for them, and re-layouts: 33 us -> 7.19 us
    while x11 -> x0, local copies, waits for them, and re-layouts: 16.5 us -> none  [the longest x3 16.5 us: attend_blocks(): state, _ = lax.scan(scan_step, state, (shaped_keys, shaped_values))]
    reduce_sum x15 -> x0, other arithmetic: 8.66 us -> none  [the longest x9 4.38 us: attend(): denominator = denominator * factor + jnp.sum(expo, axis=-1)]
    all_gather x1 -> x0, local copies, waits for them, and re-layouts: 6.66 us -> none  [per_device(): piece = lax.all_gather(text_kv_weight, 'blk', axis=0, tiled=True)]
  transfers between devices with their start and end apart: 6 -> 0, of which waited for: 6 -> 0; matrix products, arithmetic and copies ran while one was open for 11% -> 0% of each run, Pallas kernels for 0% -> 0%
where the time goes in v1:
time: 122 us
  Pallas kernels  115 us (94%)
  local copies, waits for them, and re-layouts  7.19 us (6%)
    pallas_call x1, Pallas kernels, per_device(): pl.pallas_call(kernel, out_shape=jax.ShapeDtypeStruct((ROWS, D), BF16), i...  115 us
    unnamed x15, local copies, waits for them, and re-layouts  7.19 us

profile of v1, /device:TPU:1, one launch (start us, length us, event | category | flops | bytes accessed | tf_op | source)
XLA Modules:
  0.0 121.9 jit_solution(16959914661680129697)
XLA Ops:
  0.0 0.0 copy-start
  0.0 1.7 %copy-done = bf16[384,3072]{1,0:T(8,128)(2,1)S(1)} copy-done((bf16[384,3072]{1,0:T(8,128)(2,1)S(1)}, bf16[384,3072]{1,0:T(8,128)(2,1)}, u32[]{:S(2)}) %copy-start) | copy-done | bytes 2359320
  1.7 0.0 copy-start.1
  1.7 0.9 copy-done.1
  2.6 0.0 copy-start.2
  2.6 0.9 copy-done.2
  3.5 0.0 copy-start.3
  3.5 0.8 copy-done.3
  4.3 0.0 copy-start.4
  4.3 0.8 copy-done.4
  5.1 0.0 copy-start.5
  5.1 0.7 copy-done.5
  5.8 0.0 copy-start.6
  5.8 0.7 copy-done.6
  6.5 114.7 %joint_attention.1 = bf16[32,3072]{1,0:T(8,128)(2,1)S(1)} custom-call(bf16[32,3072]{1,0:T(8,128)(2,1)S(1)} %copy-done.1, bf16[8,3072]{1,0:T(8,128)(2,1)S(1)} %copy-done.3, f32[3,3072]{1,0:T(4,128)S(1)} %copy-done.4, f32[2,3072]{1,0:T(2,128)S(1)} %copy-done.5, f32[3,128]{1,0:T(4,128)S(1)} %copy-done.6, bf16[3,3072,384]{2,1,0:T(8,128)(2,1)} %bitcast.3, ...), custom_call_target="tpu_custom_call" | custom-call | tf_op jit(solution)/shard_map/joint_attention/pallas_call | solution.py:419
  121.2 0.7 copy.10
Async XLA Ops:
  0.0 1.7 %copy-start = (bf16[384,3072]{1,0:T(8,128)(2,1)S(1)}, bf16[384,3072]{1,0:T(8,128)(2,1)}, u32[]{:S(2)}) copy-start(bf16[384,3072]{1,0:T(8,128)(2,1)} %out_hbm.1) | copy-start | bytes 7077892
  1.7 0.9 copy-start.1
  2.6 0.9 copy-start.2
  3.5 0.8 copy-start.3
  4.3 0.8 copy-start.4
  5.1 0.7 copy-start.5
  5.8 0.7 copy-start.6

commit v2 on v1

v2 whole, which is shorter than its diff:
```python
import math

import jax
import jax.numpy as jnp
from jax import lax
from jax.experimental import pallas as pl
from jax.experimental.pallas import tpu as pltpu
from jax.sharding import PartitionSpec as P

D = 3072
HEAD = 128
HEADS_HERE = 3
ROWS = 32
BLOCK = 256
PARTS = 2
PART = ROWS // PARTS
QUERIES = 1024
CAP_COLS = 96
CAP_ROWS = 8
CHUNKS = 4
CHUNK = D // CHUNKS
MESH = pl.DeviceIdType.MESH
F32 = jnp.float32
BF16 = jnp.bfloat16
QUERY_SCALE = math.log2(math.e) / math.sqrt(HEAD)
LOG2E = math.log2(math.e)
NEAR_STEPS = [(1, 0), (3, 0), (2, 0), (0, 1)]
TOKEN_HOPS = [
    (0, (1, 0)), (0, (3, 0)), (0, (2, 0)), (0, (0, 1)),
    (1, (0, 1)), (2, (0, 1)), (4, (2, 0)),
]
REDUCE_HOPS = [
    (5, (0, 1)), (6, (0, 1)), (7, (2, 0)), (3, (2, 0)),
    (1, (3, 0)), (2, (1, 0)), (4, (0, 1)),
]


def layer_norm(values, shift, scale):
    average = jnp.mean(values, axis=-1, keepdims=True)
    centered = values - average
    spread = jnp.mean(centered * centered, axis=-1, keepdims=True)
    return (centered * lax.rsqrt(spread + 1e-06) * (1.0 + scale) + shift).astype(BF16)


def root_norm(values, gain):
    squares = jnp.mean(values * values, axis=-1, keepdims=True)
    return (values * lax.rsqrt(squares + 1e-06) * gain).astype(BF16)


def kernel(
    img_hbm, text_hbm, mod_hbm, tmod_hbm, gains_hbm, qkv_hbm, tkv_hbm, out_hbm,
    out_ref,
    img_ref, text_ref, mod_ref, tmod_ref, gains_ref,
    w_qkv, w_cap, w_out, tok, a1_send, a1_recv, a2_send, a2_recv,
    part, r1_recv, r2_send, r2_recv, r3_send, r3_recv, cap_all,
    q_buf, kv, m_buf, acc, o_send, o_recv, l_send, l_recv, att, p_send, p_recv, p_keep,
    w_sem, tok_send, tok_recv, a_sems, r_sems, capall_sems,
    q_send, q_recv, right_send, right_recv, left_send, left_recv,
    o_ssem, o_rsem, l_ssem, l_rsem, p_ssem, p_rsem,
):
    u = lax.axis_index("ulysses")
    b = lax.axis_index("blk")
    y, xh = u // 2, lax.rem(u, 2)
    xl, z, c = b // 16, lax.rem(b // 2, 8), lax.rem(b, 2)

    def ulysses_peer(dy, dx):
        return lax.rem(y + dy, 4) * 2 + lax.rem(xh + dx, 2)

    def blk_of(xl_, z_, c_):
        return xl_ * 16 + z_ * 2 + c_

    def quad_peer(j):
        return {"blk": blk_of(lax.rem(xl + j // 2, 2), z, lax.rem(c + j % 2, 2))}

    def line_peer(dz):
        return {"blk": blk_of(xl, lax.rem(z + dz, 8), c)}

    load_cap = pltpu.make_async_copy(tkv_hbm, w_cap.at[:, pl.ds(0, CAP_COLS), :], w_sem.at[0])
    load_qkv = pltpu.make_async_copy(qkv_hbm, w_qkv, w_sem.at[1])
    load_out = pltpu.make_async_copy(out_hbm, w_out, w_sem.at[2])
    small = [
        pltpu.make_async_copy(src, dst, w_sem.at[3 + i])
        for i, (src, dst) in enumerate(
            [
                (img_hbm, img_ref),
                (mod_hbm, mod_ref),
                (text_hbm, text_ref),
                (tmod_hbm, tmod_ref),
                (gains_hbm, gains_ref),
            ]
        )
    ]
    for load in small:
        load.start()
    load_cap.start()
    load_qkv.start()
    load_out.start()

    barrier = pltpu.get_barrier_semaphore()
    for dy, dx in NEAR_STEPS:
        pl.semaphore_signal(
            barrier, inc=1, device_id={"ulysses": ulysses_peer(dy, dx)}, device_id_type=MESH
        )

    for j in range(1, 4):
        pl.semaphore_signal(barrier, inc=1, device_id=quad_peer(j), device_id_type=MESH)
    for dz in range(1, 8):
        pl.semaphore_signal(barrier, inc=1, device_id=line_peer(dz), device_id_type=MESH)

    small[0].wait()
    small[1].wait()
    normed = layer_norm(img_ref[...].astype(F32), mod_ref[0:1, :], mod_ref[1:2, :])
    for k in range(PARTS):
        tok[k, 0] = normed[k * PART : (k + 1) * PART]

    for load in small[2:]:
        load.wait()
    cap = layer_norm(text_ref[...].astype(F32), tmod_ref[0:1, :], tmod_ref[1:2, :]).astype(F32)
    groups = jnp.concatenate([cap[:, 384 * g : 384 * g + 384] for g in range(8)], axis=0)
    row = lax.broadcasted_iota(jnp.int32, (384, 512), 0)
    col = lax.broadcasted_iota(jnp.int32, (384, 512), 1)
    lane = lax.rem(col, 128)
    pick = jnp.where((lane < CAP_COLS) & (row == (col // 128) * CAP_COLS + lane), 1.0, 0.0)
    pieces = jnp.dot(groups.astype(BF16), pick.astype(BF16), preferred_element_type=F32)

    def piece(xl_, z_, c_):
        g, t = divmod(xl_ * 16 + z_ * 2 + c_, 4)
        return pieces[8 * g : 8 * g + 8, 128 * t : 128 * t + 128]

    for c_ in range(2):
        for xl_ in range(2):
            rows = jnp.concatenate([piece(xl_, z_, c_) for z_ in range(8)], axis=0)
            a1_send[c_ * 2 + xl_] = rows.astype(BF16)
    for h in range(HEADS_HERE):
        w_cap[h, CAP_COLS:128, :] = jnp.zeros((128 - CAP_COLS, 256), BF16)

    pl.semaphore_wait(barrier, 14)

    quad = c * 2 + xl

    def a1_copy(j):
        to = lax.rem(c + j % 2, 2) * 2 + lax.rem(xl + j // 2, 2)
        return pltpu.make_async_remote_copy(
            src_ref=a1_send.at[to], dst_ref=a1_recv.at[quad],
            send_sem=a_sems.at[0, j], recv_sem=a_sems.at[1, j],
            device_id=quad_peer(j), device_id_type=MESH,
        )

    def a2_copy(dz):
        return pltpu.make_async_remote_copy(
            src_ref=a2_send.at[lax.rem(z + dz, 8)], dst_ref=a2_recv.at[z],
            send_sem=a_sems.at[2, dz], recv_sem=a_sems.at[3, dz],
            device_id=line_peer(dz), device_id_type=MESH,
        )

    def token_copy(k, i):
        source, (dy, dx) = TOKEN_HOPS[i]
        return pltpu.make_async_remote_copy(
            src_ref=tok.at[k, source], dst_ref=tok.at[k, i + 1],
            send_sem=tok_send.at[k, i], recv_sem=tok_recv.at[k, i],
            device_id={"ulysses": ulysses_peer(dy, dx)}, device_id_type=MESH,
        )

    def token_near(k):
        for i in (3, 0, 1):
            token_copy(k, i).start()

    def token_onward(k):
        for source, onward in ((0, 4), (1, 5), (3, 6)):
            token_copy(k, source).wait_recv()
            token_copy(k, onward).start()
        token_copy(k, 2).start()

    def token_rest(k):
        for i in (2, 4, 5, 6):
            token_copy(k, i).wait_recv()

    for j in range(1, 4):
        a1_copy(j).start()
    token_near(0)

    a1_recv[quad] = a1_send[quad]
    for j in range(1, 4):
        a1_copy(j).wait_recv()
    by_quad = a1_recv[...].astype(F32)
    for z_ in range(8):
        rows = jnp.concatenate([by_quad[i, 8 * z_ : 8 * z_ + 8] for i in range(4)], axis=0)
        a2_send[z_] = rows.astype(BF16)
    for dz in range(1, 8):
        a2_copy(dz).start()
    a2_recv[z] = a2_send[z]

    token_onward(0)
    token_near(1)

    load_cap.wait()
    for dz in range(1, 8):
        a2_copy(dz).wait_recv()
    cap_rows = a2_recv[...].reshape(256, 128)
    for h in range(HEADS_HERE):
        product = jnp.dot(cap_rows, w_cap[h], preferred_element_type=F32)
        both = jnp.concatenate(
            [product[:, :128].reshape(8, 4, 8, 128), product[:, 128:].reshape(8, 4, 8, 128)],
            axis=2,
        )
        for i in range(4):
            part[i, :, :, h * 128 : (h + 1) * 128] = both[:, i].astype(BF16)

    other_c, other_xl = lax.rem(c + 1, 2), lax.rem(xl + 1, 2)
    r1_copy = pltpu.make_async_remote_copy(
        src_ref=part.at[pl.ds(other_c * 2, 2)], dst_ref=r1_recv,
        send_sem=r_sems.at[0, 0], recv_sem=r_sems.at[1, 0],
        device_id=quad_peer(1), device_id_type=MESH,
    )
    r1_copy.start()
    r2_copy = pltpu.make_async_remote_copy(
        src_ref=r2_send, dst_ref=r2_recv,
        send_sem=r_sems.at[0, 1], recv_sem=r_sems.at[1, 1],
        device_id=quad_peer(2), device_id_type=MESH,
    )

    def r3_copy(dz):
        return pltpu.make_async_remote_copy(
            src_ref=r3_send.at[lax.rem(z + dz, 8)], dst_ref=r3_recv.at[z],
            send_sem=r_sems.at[2, dz], recv_sem=r_sems.at[3, dz],
            device_id=line_peer(dz), device_id_type=MESH,
        )

    def capall_copy(dz):
        return pltpu.make_async_remote_copy(
            src_ref=cap_all.at[0], dst_ref=cap_all.at[dz],
            send_sem=capall_sems.at[0, dz], recv_sem=capall_sems.at[1, dz],
            device_id=line_peer(dz), device_id_type=MESH,
        )

    token_rest(0)
    token_onward(1)

    def ring_right(k, h, s):
        src, dst = kv.at[h, s - 1, k], kv.at[h, s, k]
        if s == 4:
            src, dst = src.at[0], dst.at[0]
        return pltpu.make_async_remote_copy(
            src_ref=src, dst_ref=dst, send_sem=right_send.at[k, h, s - 1],
            recv_sem=right_recv.at[k, h, s - 1], device_id=line_peer(1), device_id_type=MESH,
        )

    def ring_left(k, h, s):
        src, dst = kv.at[h, (9 - s) % 8, k], kv.at[h, 8 - s, k]
        if s == 4:
            src, dst = src.at[1], dst.at[1]
        return pltpu.make_async_remote_copy(
            src_ref=src, dst_ref=dst, send_sem=left_send.at[k, h, s - 1],
            recv_sem=left_recv.at[k, h, s - 1], device_id=line_peer(7), device_id_type=MESH,
        )

    def query_copy(h, j):
        return pltpu.make_async_remote_copy(
            src_ref=q_buf.at[h, 0], dst_ref=q_buf.at[h, j],
            send_sem=q_send.at[h, j], recv_sem=q_recv.at[h, j],
            device_id=quad_peer(j), device_id_type=MESH,
        )

    def project(k):
        def head(h, carry):
            rows = tok[k].reshape(PART * 8, D)
            projected = jnp.dot(rows, w_qkv[h], preferred_element_type=F32)
            kv[h, 0, k, 0] = root_norm(projected[:, 128:256], gains_ref[1:2, :])
            kv[h, 0, k, 1] = projected[:, 256:384].astype(BF16)
            ring_right(k, h, 1).start()
            ring_left(k, h, 1).start()
            q_buf[h, 0, k] = root_norm(projected[:, 0:128], gains_ref[0:1, :] * QUERY_SCALE)
            if k == PARTS - 1:
                for j in range(1, 4):
                    query_copy(h, j).start()
            return carry

        lax.fori_loop(0, HEADS_HERE, head, 0)

    load_qkv.wait()
    project(0)

    r1_copy.wait_recv()
    r2_send[...] = (part[c * 2 + other_xl].astype(F32) + r1_recv[other_xl].astype(F32)).astype(BF16)
    r2_copy.start()

    token_rest(1)
    project(1)

    r2_copy.wait_recv()
    r3_send[...] = (
        part[quad].astype(F32) + r1_recv[xl].astype(F32) + r2_recv[...].astype(F32)
    ).astype(BF16)
    for dz in range(1, 8):
        r3_copy(dz).start()
    r3_recv[z] = r3_send[z]

    def attend(h, slots, first=False, caption=None):
        q = q_buf[h].reshape(QUERIES, HEAD)
        keys = [jnp.concatenate([kv[h, s, k, 0] for k in range(PARTS)], axis=0) for s in slots]
        values = [jnp.concatenate([kv[h, s, k, 1] for k in range(PARTS)], axis=0) for s in slots]
        if caption is not None:
            keys.append(caption[0])
            values.append(caption[1])
        scores = [
            lax.dot_general(q, k, (((1,), (1,)), ((), ())), preferred_element_type=F32)
            for k in keys
        ]
        halves = [s[:, i : i + 128] for s in scores for i in range(0, s.shape[1], 128)]
        top = halves[0]
        for s in halves[1 : 2 * len(slots)]:
            top = jnp.maximum(top, s)
        top = jnp.max(top, axis=-1, keepdims=True)
        for s in halves[2 * len(slots) :]:
            top = jnp.maximum(top, jnp.max(s, axis=-1, keepdims=True))
        if first:
            m_new = jnp.broadcast_to(top, (QUERIES, 128))
        else:
            m_old = m_buf[h]
            m_new = jnp.maximum(m_old, top)
        wide = jnp.concatenate([m_new, m_new], axis=1)
        update = None
        for s, v in zip(scores, values):
            weights = jnp.exp2(s - wide[:, : s.shape[1]]).astype(BF16)
            filled = jnp.concatenate([v, jnp.ones(v.shape, BF16)], axis=1)
            term = jnp.dot(weights, filled, preferred_element_type=F32)
            update = term if update is None else update + term
        if first:
            acc[h] = update
        else:
            alpha = jnp.exp2(m_old - m_new)
            acc[h] = acc[h] * jnp.concatenate([alpha, alpha], axis=1) + update
        m_buf[h] = m_new

    def forward(k, h, s):
        ring_right(k, h, s - 1).wait_recv()
        ring_right(k, h, s).start()
        ring_left(k, h, s - 1).wait_recv()
        ring_left(k, h, s).start()

    def step_two(h, carry):
        forward(0, h, 2)
        return carry

    lax.fori_loop(0, HEADS_HERE, step_two, 0)

    for dz in range(1, 8):
        r3_copy(dz).wait_recv()
    total = jnp.sum(r3_recv[...].astype(F32), axis=0)
    for h in range(HEADS_HERE):
        cols = slice(h * 128, (h + 1) * 128)
        key_rows = root_norm(total[0:8, cols], gains_ref[2:3, :]).astype(F32)
        cap_all[0, :, cols] = jnp.concatenate([key_rows, total[8:16, cols]], axis=0).astype(BF16)
    for dz in range(1, 8):
        capall_copy(dz).start()

    def step_two_more(h, carry):
        forward(1, h, 2)
        return carry

    lax.fori_loop(0, HEADS_HERE, step_two_more, 0)

    def step_three_first(h, carry):
        forward(0, h, 3)
        return carry

    lax.fori_loop(0, HEADS_HERE, step_three_first, 0)

    def step_three(h, carry):
        forward(1, h, 3)
        for j in range(1, 4):
            query_copy(h, j).wait_recv()
        attend(h, [0, 1, 7], first=True)
        return carry

    lax.fori_loop(0, HEADS_HERE, step_three, 0)

    for dz in range(1, 8):
        capall_copy(dz).wait_recv()

    def step_four_first(h, carry):
        forward(0, h, 4)
        return carry

    lax.fori_loop(0, HEADS_HERE, step_four_first, 0)

    def step_four(h, carry):
        forward(1, h, 4)
        col = pl.ds(pl.multiple_of(h * 128, 128), 128)
        cap_kv = cap_all[:, :, col].astype(F32)
        cap_keys = cap_kv[:, 0:8, :].reshape(64, 128).astype(BF16)
        cap_values = cap_kv[:, 8:16, :].reshape(64, 128).astype(BF16)
        attend(h, [2, 6], caption=(cap_keys, cap_values))
        attend(h, [3, 5])
        return carry

    lax.fori_loop(0, HEADS_HERE, step_four, 0)

    def o_copy(h, j):
        return pltpu.make_async_remote_copy(
            src_ref=o_send.at[h, j], dst_ref=o_recv.at[h, j],
            send_sem=o_ssem.at[h, j], recv_sem=o_rsem.at[h, j],
            device_id=quad_peer(j), device_id_type=MESH,
        )

    def l_copy(h, j):
        return pltpu.make_async_remote_copy(
            src_ref=l_send.at[h, j], dst_ref=l_recv.at[h, j],
            send_sem=l_ssem.at[h, j], recv_sem=l_rsem.at[h, j],
            device_id=quad_peer(j), device_id_type=MESH,
        )

    def step_last(h, carry):
        for k in range(PARTS):
            ring_right(k, h, 4).wait_recv()
            ring_left(k, h, 4).wait_recv()
        attend(h, [4])
        for j in range(1, 4):
            rows = slice(j * BLOCK, (j + 1) * BLOCK)
            denominator = acc[h, rows, 128:]
            o_send[h, j] = (acc[h, rows, :128] / denominator).astype(BF16)
            level = m_buf[h, rows, :] + jnp.log(denominator) * LOG2E
            l_send[h, j] = level.T[0:8, :]
            o_copy(h, j).start()
            l_copy(h, j).start()
        return carry

    lax.fori_loop(0, HEADS_HERE, step_last, 0)

    def combine(h, carry):
        denominator = acc[h, 0:BLOCK, 128:]
        outs = [acc[h, 0:BLOCK, :128] / denominator]
        levels = [m_buf[h, 0:BLOCK, :] + jnp.log(denominator) * LOG2E]
        for j in range(1, 4):
            o_copy(h, j).wait_recv()
            l_copy(h, j).wait_recv()
            outs.append(o_recv[h, j].astype(F32))
            levels.append(jnp.broadcast_to(l_recv[h, j][0:1, :], (128, BLOCK)).T)
        top = levels[0]
        for level in levels[1:]:
            top = jnp.maximum(top, level)
        numerator, weight = None, None
        for out, level in zip(outs, levels):
            share = jnp.exp2(level - top)
            numerator = out * share if numerator is None else numerator + out * share
            weight = share if weight is None else weight + share
        att[h] = (numerator / weight).astype(BF16)
        return carry

    lax.fori_loop(0, HEADS_HERE, combine, 0)

    load_out.wait()

    def p_copy(n, i):
        source, (dy, dx) = REDUCE_HOPS[i]
        return pltpu.make_async_remote_copy(
            src_ref=p_send.at[n, source], dst_ref=p_recv.at[n, i],
            send_sem=p_ssem.at[n, i], recv_sem=p_rsem.at[n, i],
            device_id={"ulysses": ulysses_peer(dy, dx)}, device_id_type=MESH,
        )

    def out_chunk(n, carry):
        cols = pl.ds(pl.multiple_of(n * CHUNK, 128), CHUNK)
        rows = jnp.concatenate([att[h] for h in range(HEADS_HERE)], axis=1)
        product = jnp.dot(rows, w_out[:, cols], preferred_element_type=F32)
        product = product.reshape(PARTS, 8, PART, CHUNK)
        for i in (5, 6, 7, 3):
            p_send[n, i] = product[:, i].reshape(ROWS, CHUNK).astype(BF16)
        for i in range(4):
            p_copy(n, i).start()
        for k, i in enumerate((0, 1, 2, 4)):
            p_keep[n, k] = product[:, i].reshape(ROWS, CHUNK)
        return carry

    lax.fori_loop(0, CHUNKS, out_chunk, 0)

    def pass_on(n, carry):
        for k, i in ((1, 0), (2, 1), (3, 2)):
            p_copy(n, i).wait_recv()
            source = REDUCE_HOPS[i + 4][0]
            p_send[n, source] = (p_keep[n, k] + p_recv[n, i].astype(F32)).astype(BF16)
            p_copy(n, i + 4).start()
        return carry

    lax.fori_loop(0, CHUNKS, pass_on, 0)

    def finish(n, carry):
        cols = pl.ds(pl.multiple_of(n * CHUNK, 128), CHUNK)
        for i in range(3, 7):
            p_copy(n, i).wait_recv()
        projection = p_keep[n, 0] + jnp.sum(p_recv[n, 3:7].astype(F32), axis=0)
        out_ref[:, cols] = (
            img_ref[:, cols].astype(F32) + mod_ref[2:3, cols] * projection
        ).astype(BF16)
        return carry

    lax.fori_loop(0, CHUNKS, finish, 0)

    for j in range(1, 4):
        a1_copy(j).wait_send()
    r1_copy.wait_send()
    r2_copy.wait_send()
    for dz in range(1, 8):
        a2_copy(dz).wait_send()
        r3_copy(dz).wait_send()
        capall_copy(dz).wait_send()
    for k in range(PARTS):
        for i in range(7):
            token_copy(k, i).wait_send()

    def drain_head(h, carry):
        for s in range(1, 5):
            for k in range(PARTS):
                ring_right(k, h, s).wait_send()
                ring_left(k, h, s).wait_send()
        for j in range(1, 4):
            query_copy(h, j).wait_send()
            o_copy(h, j).wait_send()
            l_copy(h, j).wait_send()
        return carry

    lax.fori_loop(0, HEADS_HERE, drain_head, 0)

    def drain_chunk(n, carry):
        for i in range(7):
            p_copy(n, i).wait_send()
        return carry

    lax.fori_loop(0, CHUNKS, drain_chunk, 0)


def per_device(
    image_tokens, text_tokens, modulation, text_modulation, norm_gains,
    qkv_weight, text_kv_weight, out_weight,
):
    qkv = jnp.transpose(qkv_weight, (1, 0, 2))
    tkv = jnp.transpose(text_kv_weight, (1, 0, 2))
    dma = pltpu.SemaphoreType.DMA
    vmem = pl.BlockSpec(memory_space=pltpu.VMEM)
    hbm = pl.BlockSpec(memory_space=pl.ANY)
    h3 = HEADS_HERE
    return pl.pallas_call(
        kernel,
        out_shape=jax.ShapeDtypeStruct((ROWS, D), BF16),
        in_specs=[hbm] * 8,
        out_specs=vmem,
        scratch_shapes=[
            pltpu.VMEM((ROWS, D), BF16),
            pltpu.VMEM((CAP_ROWS, D), BF16),
            pltpu.VMEM((3, D), F32),
            pltpu.VMEM((2, D), F32),
            pltpu.VMEM((3, HEAD), F32),
            pltpu.VMEM((h3, D, 384), BF16),
            pltpu.VMEM((h3, 128, 256), BF16),
            pltpu.VMEM((384, D), BF16),
            pltpu.VMEM((PARTS, 8, PART, D), BF16),
            pltpu.VMEM((4, 64, 128), BF16),
            pltpu.VMEM((4, 64, 128), BF16),
            pltpu.VMEM((8, 32, 128), BF16),
            pltpu.VMEM((8, 32, 128), BF16),
            pltpu.VMEM((4, 8, 16, 384), BF16),
            pltpu.VMEM((2, 8, 16, 384), BF16),
            pltpu.VMEM((8, 16, 384), BF16),
            pltpu.VMEM((8, 16, 384), BF16),
            pltpu.VMEM((8, 16, 384), BF16),
            pltpu.VMEM((8, 16, 384), BF16),
            pltpu.VMEM((8, 16, 384), BF16),
            pltpu.VMEM((h3, 4, PARTS, BLOCK // PARTS, 128), BF16),
            pltpu.VMEM((h3, 8, PARTS, 2, BLOCK // PARTS, 128), BF16),
            pltpu.VMEM((h3, QUERIES, 128), F32),
            pltpu.VMEM((h3, QUERIES, 256), F32),
            pltpu.VMEM((h3, 4, BLOCK, 128), BF16),
            pltpu.VMEM((h3, 4, BLOCK, 128), BF16),
            pltpu.VMEM((h3, 4, 8, BLOCK), F32),
            pltpu.VMEM((h3, 4, 8, BLOCK), F32),
            pltpu.VMEM((h3, BLOCK, 128), BF16),
            pltpu.VMEM((CHUNKS, 8, ROWS, CHUNK), BF16),
            pltpu.VMEM((CHUNKS, 7, ROWS, CHUNK), BF16),
            pltpu.VMEM((CHUNKS, 4, ROWS, CHUNK), F32),
            dma((8,)), dma((PARTS, 7)), dma((PARTS, 7)), dma((4, 8)), dma((4, 8)), dma((2, 8)),
            dma((h3, 4)), dma((h3, 4)),
            dma((PARTS, h3, 4)), dma((PARTS, h3, 4)), dma((PARTS, h3, 4)), dma((PARTS, h3, 4)),
            dma((h3, 4)), dma((h3, 4)), dma((h3, 4)), dma((h3, 4)),
            dma((CHUNKS, 7)), dma((CHUNKS, 7)),
        ],
        compiler_params=pltpu.CompilerParams(
            collective_id=0, has_side_effects=True, vmem_limit_bytes=60 * 1024 * 1024
        ),
        name="joint_attention",
    )(image_tokens, text_tokens, modulation, text_modulation, norm_gains, qkv, tkv, out_weight)


def solution(mesh):
    in_specs = (
        P(("blk", "ulysses"), None),
        P("blk", None),
        P(),
        P(),
        P(),
        P(None, "ulysses", None),
        P("blk", "ulysses", None),
        P("ulysses", None),
    )
    out_specs = P(("blk", "ulysses"), None)
    return jax.shard_map(
        per_device, mesh=mesh, in_specs=in_specs, out_specs=out_specs, check_vma=False
    )
```

time: 122 us -> 91.8 us (0.75)
  Pallas kernels: 115 us -> 90.1 us
  local copies, waits for them, and re-layouts: 7.19 us -> 1.62 us
    pallas_call x1, Pallas kernels: 115 us -> 90.1 us  [per_device(): pl.pallas_call(kernel, out_shape=jax.ShapeDtypeStruct((ROWS, D), BF16), i...]
    unnamed x15 -> x1, local copies, waits for them, and re-layouts: 7.19 us -> 1.62 us
where the time goes in v2:
time: 91.8 us; the launch traced here: 91.7 us
  Pallas kernels  90.1 us (98%)
  local copies, waits for them, and re-layouts  1.62 us (2%)
    pallas_call x1, Pallas kernels, per_device(): pl.pallas_call(kernel, out_shape=jax.ShapeDtypeStruct((ROWS, D), BF16), i...  90.1 us

profile of v2, /device:TPU:1, one launch (start us, length us, event | category | flops | bytes accessed | tf_op | source)
XLA Modules:
  0.0 91.7 jit_solution(16397157258803274377)
XLA Ops:
  0.0 90.1 %joint_attention.1 = bf16[32,3072]{1,0:T(8,128)(2,1)} custom-call(bf16[32,3072]{1,0:T(8,128)(2,1)} %img_hbm.1, bf16[8,3072]{1,0:T(8,128)(2,1)} %text_hbm.1, f32[3,3072]{1,0:T(4,128)} %mod_hbm.1, f32[2,3072]{1,0:T(2,128)} %tmod_hbm.1, f32[3,128]{1,0:T(4,128)} %gains_hbm.1, bf16[3,3072,384]{2,1,0:T(8,128)(2,1)} %bitcast.2, bf16[3,96,256]{2,1,0:T(8,128)(2,1)} %bitcast.3, ...), custom_call_target="tpu_custom_call" | custom-call | tf_op jit(solution)/shard_map/joint_attention/pallas_call | solution.py:542
  90.1 1.6 %copy.10 = bf16[32,3072]{1,0:T(8,128)(2,1)} copy(bf16[32,3072]{1,0:T(8,128)(2,1)} %joint_attention.1) | data formatting | bytes 393216

commit v3 on v2

--- a/solution.py
+++ b/solution.py
@@ -53,10 +53,10 @@
     img_ref, text_ref, mod_ref, tmod_ref, gains_ref,
     w_qkv, w_cap, w_out, tok, a1_send, a1_recv, a2_send, a2_recv,
     part, r1_recv, r2_send, r2_recv, r3_send, r3_recv, cap_all,
-    q_buf, kv, m_buf, acc, o_send, o_recv, l_send, l_recv, att, p_send, p_recv, p_keep,
+    q_buf, kv, m_buf, acc, o_send, o_recv, l_send, l_recv, ox_send, ox_recv, lx_send, lx_recv, att, p_send, p_recv, p_keep,
     w_sem, tok_send, tok_recv, a_sems, r_sems, capall_sems,
     q_send, q_recv, right_send, right_recv, left_send, left_recv,
-    o_ssem, o_rsem, l_ssem, l_rsem, p_ssem, p_rsem,
+    o_ssem, o_rsem, p_ssem, p_rsem,
 ):
     u = lax.axis_index("ulysses")
     b = lax.axis_index("blk")
@@ -119,8 +119,8 @@
     groups = jnp.concatenate([cap[:, 384 * g : 384 * g + 384] for g in range(8)], axis=0)
     row = lax.broadcasted_iota(jnp.int32, (384, 512), 0)
     col = lax.broadcasted_iota(jnp.int32, (384, 512), 1)
-    lane = lax.rem(col, 128)
-    pick = jnp.where((lane < CAP_COLS) & (row == (col // 128) * CAP_COLS + lane), 1.0, 0.0)
+    lane = col & 127
+    pick = jnp.where((lane < CAP_COLS) & (row == (col >> 7) * CAP_COLS + lane), 1.0, 0.0)
     pieces = jnp.dot(groups.astype(BF16), pick.astype(BF16), preferred_element_type=F32)
 
     def piece(xl_, z_, c_):
@@ -179,40 +179,12 @@
         a1_copy(j).start()
     token_near(0)
 
-    a1_recv[quad] = a1_send[quad]
-    for j in range(1, 4):
-        a1_copy(j).wait_recv()
-    by_quad = a1_recv[...].astype(F32)
-    for z_ in range(8):
-        rows = jnp.concatenate([by_quad[i, 8 * z_ : 8 * z_ + 8] for i in range(4)], axis=0)
-        a2_send[z_] = rows.astype(BF16)
-    for dz in range(1, 8):
-        a2_copy(dz).start()
-    a2_recv[z] = a2_send[z]
-
-    token_onward(0)
-    token_near(1)
-
-    load_cap.wait()
-    for dz in range(1, 8):
-        a2_copy(dz).wait_recv()
-    cap_rows = a2_recv[...].reshape(256, 128)
-    for h in range(HEADS_HERE):
-        product = jnp.dot(cap_rows, w_cap[h], preferred_element_type=F32)
-        both = jnp.concatenate(
-            [product[:, :128].reshape(8, 4, 8, 128), product[:, 128:].reshape(8, 4, 8, 128)],
-            axis=2,
-        )
-        for i in range(4):
-            part[i, :, :, h * 128 : (h + 1) * 128] = both[:, i].astype(BF16)
-
     other_c, other_xl = lax.rem(c + 1, 2), lax.rem(xl + 1, 2)
     r1_copy = pltpu.make_async_remote_copy(
         src_ref=part.at[pl.ds(other_c * 2, 2)], dst_ref=r1_recv,
         send_sem=r_sems.at[0, 0], recv_sem=r_sems.at[1, 0],
         device_id=quad_peer(1), device_id_type=MESH,
     )
-    r1_copy.start()
     r2_copy = pltpu.make_async_remote_copy(
         src_ref=r2_send, dst_ref=r2_recv,
         send_sem=r_sems.at[0, 1], recv_sem=r_sems.at[1, 1],
@@ -233,9 +205,6 @@
             device_id=line_peer(dz), device_id_type=MESH,
         )
 
-    token_rest(0)
-    token_onward(1)
-
     def ring_right(k, h, s):
         src, dst = kv.at[h, s - 1, k], kv.at[h, s, k]
         if s == 4:
@@ -260,6 +229,12 @@
             send_sem=q_send.at[h, j], recv_sem=q_recv.at[h, j],
             device_id=quad_peer(j), device_id_type=MESH,
         )
+
+    def forward(k, h, s):
+        ring_right(k, h, s - 1).wait_recv()
+        ring_right(k, h, s).start()
+        ring_left(k, h, s - 1).wait_recv()
+        ring_left(k, h, s).start()
 
     def project(k):
         def head(h, carry):
@@ -277,23 +252,64 @@
 
         lax.fori_loop(0, HEADS_HERE, head, 0)
 
-    load_qkv.wait()
-    project(0)
-
-    r1_copy.wait_recv()
-    r2_send[...] = (part[c * 2 + other_xl].astype(F32) + r1_recv[other_xl].astype(F32)).astype(BF16)
-    r2_copy.start()
-
-    token_rest(1)
-    project(1)
-
-    r2_copy.wait_recv()
-    r3_send[...] = (
-        part[quad].astype(F32) + r1_recv[xl].astype(F32) + r2_recv[...].astype(F32)
-    ).astype(BF16)
-    for dz in range(1, 8):
-        r3_copy(dz).start()
-    r3_recv[z] = r3_send[z]
+    def cap_columns():
+        a1_recv[quad] = a1_send[quad]
+        for j in range(1, 4):
+            a1_copy(j).wait_recv()
+        by_quad = a1_recv[...].astype(F32)
+        for z_ in range(8):
+            rows = jnp.concatenate([by_quad[i, 8 * z_ : 8 * z_ + 8] for i in range(4)], axis=0)
+            a2_send[z_] = rows.astype(BF16)
+        for dz in range(1, 8):
+            a2_copy(dz).start()
+        a2_recv[z] = a2_send[z]
+
+    def cap_partial():
+        load_cap.wait()
+        for dz in range(1, 8):
+            a2_copy(dz).wait_recv()
+        cap_rows = a2_recv[...].reshape(256, 128)
+        for h in range(HEADS_HERE):
+            product = jnp.dot(cap_rows, w_cap[h], preferred_element_type=F32)
+            both = jnp.concatenate(
+                [product[:, :128].reshape(8, 4, 8, 128), product[:, 128:].reshape(8, 4, 8, 128)],
+                axis=2,
+            )
+            for i in range(4):
+                part[i, :, :, h * 128 : (h + 1) * 128] = both[:, i].astype(BF16)
+        r1_copy.start()
+
+    def cap_cores():
+        r1_copy.wait_recv()
+        r2_send[...] = (part[c * 2 + other_xl].astype(F32) + r1_recv[other_xl].astype(F32)).astype(BF16)
+        r2_copy.start()
+
+    def cap_x():
+        r2_copy.wait_recv()
+        r3_send[...] = (
+            part[quad].astype(F32) + r1_recv[xl].astype(F32) + r2_recv[...].astype(F32)
+        ).astype(BF16)
+        for dz in range(1, 8):
+            r3_copy(dz).start()
+        r3_recv[z] = r3_send[z]
+
+    def cap_line():
+        for dz in range(1, 8):
+            r3_copy(dz).wait_recv()
+        total = jnp.sum(r3_recv[...].astype(F32), axis=0)
+        for h in range(HEADS_HERE):
+            cols = slice(h * 128, (h + 1) * 128)
+            key_rows = root_norm(total[0:8, cols], gains_ref[2:3, :]).astype(F32)
+            cap_all[0, :, cols] = jnp.concatenate([key_rows, total[8:16, cols]], axis=0).astype(BF16)
+        for dz in range(1, 8):
+            capall_copy(dz).start()
+
+    def forward_all(k, s):
+        def head(h, carry):
+            forward(k, h, s)
+            return carry
+
+        lax.fori_loop(0, HEADS_HERE, head, 0)
 
     def attend(h, slots, first=False, caption=None):
         q = q_buf[h].reshape(QUERIES, HEAD)
@@ -332,39 +348,22 @@
             acc[h] = acc[h] * jnp.concatenate([alpha, alpha], axis=1) + update
         m_buf[h] = m_new
 
-    def forward(k, h, s):
-        ring_right(k, h, s - 1).wait_recv()
-        ring_right(k, h, s).start()
-        ring_left(k, h, s - 1).wait_recv()
-        ring_left(k, h, s).start()
-
-    def step_two(h, carry):
-        forward(0, h, 2)
-        return carry
-
-    lax.fori_loop(0, HEADS_HERE, step_two, 0)
-
-    for dz in range(1, 8):
-        r3_copy(dz).wait_recv()
-    total = jnp.sum(r3_recv[...].astype(F32), axis=0)
-    for h in range(HEADS_HERE):
-        cols = slice(h * 128, (h + 1) * 128)
-        key_rows = root_norm(total[0:8, cols], gains_ref[2:3, :]).astype(F32)
-        cap_all[0, :, cols] = jnp.concatenate([key_rows, total[8:16, cols]], axis=0).astype(BF16)
-    for dz in range(1, 8):
-        capall_copy(dz).start()
-
-    def step_two_more(h, carry):
-        forward(1, h, 2)
-        return carry
-
-    lax.fori_loop(0, HEADS_HERE, step_two_more, 0)
-
-    def step_three_first(h, carry):
-        forward(0, h, 3)
-        return carry
-
-    lax.fori_loop(0, HEADS_HERE, step_three_first, 0)
+    token_onward(0)
+    cap_columns()
+    cap_partial()
+    token_rest(0)
+    token_near(1)
+    load_qkv.wait()
+    cap_cores()
+    project(0)
+    token_onward(1)
+    cap_x()
+    forward_all(0, 2)
+    token_rest(1)
+    project(1)
+    cap_line()
+    forward_all(1, 2)
+    forward_all(0, 3)
 
     def step_three(h, carry):
         forward(1, h, 3)
@@ -375,14 +374,9 @@
 
     lax.fori_loop(0, HEADS_HERE, step_three, 0)
 
+    forward_all(0, 4)
     for dz in range(1, 8):
         capall_copy(dz).wait_recv()
-
-    def step_four_first(h, carry):
-        forward(0, h, 4)
-        return carry
-
-    lax.fori_loop(0, HEADS_HERE, step_four_first, 0)
 
     def step_four(h, carry):
         forward(1, h, 4)
@@ -396,55 +390,92 @@
 
     lax.fori_loop(0, HEADS_HERE, step_four, 0)
 
-    def o_copy(h, j):
-        return pltpu.make_async_remote_copy(
-            src_ref=o_send.at[h, j], dst_ref=o_recv.at[h, j],
-            send_sem=o_ssem.at[h, j], recv_sem=o_rsem.at[h, j],
-            device_id=quad_peer(j), device_id_type=MESH,
-        )
-
-    def l_copy(h, j):
-        return pltpu.make_async_remote_copy(
-            src_ref=l_send.at[h, j], dst_ref=l_recv.at[h, j],
-            send_sem=l_ssem.at[h, j], recv_sem=l_rsem.at[h, j],
-            device_id=quad_peer(j), device_id_type=MESH,
-        )
-
-    def step_last(h, carry):
+    def core_copy(h):
+        return pltpu.make_async_remote_copy(
+            src_ref=o_send.at[h], dst_ref=o_recv.at[h],
+            send_sem=o_ssem.at[h, 0], recv_sem=o_rsem.at[h, 0],
+            device_id=quad_peer(1), device_id_type=MESH,
+        )
+
+    def core_level_copy(h):
+        return pltpu.make_async_remote_copy(
+            src_ref=l_send.at[h], dst_ref=l_recv.at[h],
+            send_sem=o_ssem.at[h, 1], recv_sem=o_rsem.at[h, 1],
+            device_id=quad_peer(1), device_id_type=MESH,
+        )
+
+    def x_copy(h):
+        return pltpu.make_async_remote_copy(
+            src_ref=ox_send.at[h], dst_ref=ox_recv.at[h],
+            send_sem=o_ssem.at[h, 2], recv_sem=o_rsem.at[h, 2],
+            device_id=quad_peer(2), device_id_type=MESH,
+        )
+
+    def x_level_copy(h):
+        return pltpu.make_async_remote_copy(
+            src_ref=lx_send.at[h], dst_ref=lx_recv.at[h],
+            send_sem=o_ssem.at[h, 3], recv_sem=o_rsem.at[h, 3],
+            device_id=quad_peer(2), device_id_type=MESH,
+        )
+
+    def partial_output(h, j):
+        rows = slice(j * BLOCK, (j + 1) * BLOCK)
+        denominator = acc[h, rows, 128:]
+        return acc[h, rows, :128] / denominator, m_buf[h, rows, :] + jnp.log(denominator) * LOG2E
+
+    def wide_level(level):
+        return jnp.broadcast_to(level[0:1, :], (128, BLOCK)).T
+
+    def merge(terms):
+        top = terms[0][1]
+        for _, level in terms[1:]:
+            top = jnp.maximum(top, level)
+        numerator, weight = None, None
+        for out, level in terms:
+            share = jnp.exp2(level - top)
+            numerator = out * share if numerator is None else numerator + out * share
+            weight = share if weight is None else weight + share
+        return (numerator / weight).astype(BF16), top, weight
+
+    def step_last(h):
         for k in range(PARTS):
             ring_right(k, h, 4).wait_recv()
             ring_left(k, h, 4).wait_recv()
         attend(h, [4])
-        for j in range(1, 4):
-            rows = slice(j * BLOCK, (j + 1) * BLOCK)
-            denominator = acc[h, rows, 128:]
-            o_send[h, j] = (acc[h, rows, :128] / denominator).astype(BF16)
-            level = m_buf[h, rows, :] + jnp.log(denominator) * LOG2E
-            l_send[h, j] = level.T[0:8, :]
-            o_copy(h, j).start()
-            l_copy(h, j).start()
-        return carry
-
-    lax.fori_loop(0, HEADS_HERE, step_last, 0)
+        for i, j in enumerate((1, 3)):
+            out, level = partial_output(h, j)
+            o_send[h, i] = out.astype(BF16)
+            l_send[h, i] = level.T[0:8, :]
+        core_copy(h).start()
+        core_level_copy(h).start()
+
+    def step_pair(h):
+        core_copy(h).wait_recv()
+        core_level_copy(h).wait_recv()
+        out, top, weight = merge(
+            [partial_output(h, 2), (o_recv[h, 1].astype(F32), wide_level(l_recv[h, 1]))]
+        )
+        ox_send[h] = out
+        lx_send[h] = (top + jnp.log(weight) * LOG2E).T[0:8, :]
+        x_copy(h).start()
+        x_level_copy(h).start()
+
+    for h in range(HEADS_HERE):
+        step_last(h)
+        if h > 0:
+            step_pair(h - 1)
+    step_pair(HEADS_HERE - 1)
 
     def combine(h, carry):
-        denominator = acc[h, 0:BLOCK, 128:]
-        outs = [acc[h, 0:BLOCK, :128] / denominator]
-        levels = [m_buf[h, 0:BLOCK, :] + jnp.log(denominator) * LOG2E]
-        for j in range(1, 4):
-            o_copy(h, j).wait_recv()
-            l_copy(h, j).wait_recv()
-            outs.append(o_recv[h, j].astype(F32))
-            levels.append(jnp.broadcast_to(l_recv[h, j][0:1, :], (128, BLOCK)).T)
-        top = levels[0]
-        for level in levels[1:]:
-            top = jnp.maximum(top, level)
-        numerator, weight = None, None
-        for out, level in zip(outs, levels):
-            share = jnp.exp2(level - top)
-            numerator = out * share if numerator is None else numerator + out * share
-            weight = share if weight is None else weight + share
-        att[h] = (numerator / weight).astype(BF16)
+        x_copy(h).wait_recv()
+        x_level_copy(h).wait_recv()
+        att[h] = merge(
+            [
+                partial_output(h, 0),
+                (o_recv[h, 0].astype(F32), wide_level(l_recv[h, 0])),
+                (ox_recv[h].astype(F32), wide_level(lx_recv[h])),
+            ]
+        )[0]
         return carry
 
     lax.fori_loop(0, HEADS_HERE, combine, 0)
@@ -515,8 +546,10 @@
                 ring_left(k, h, s).wait_send()
         for j in range(1, 4):
             query_copy(h, j).wait_send()
-            o_copy(h, j).wait_send()
-            l_copy(h, j).wait_send()
+        core_copy(h).wait_send()
+        core_level_copy(h).wait_send()
+        x_copy(h).wait_send()
+        x_level_copy(h).wait_send()
         return carry
 
     lax.fori_loop(0, HEADS_HERE, drain_head, 0)
@@ -569,10 +602,14 @@
             pltpu.VMEM((h3, 8, PARTS, 2, BLOCK // PARTS, 128), BF16),
             pltpu.VMEM((h3, QUERIES, 128), F32),
             pltpu.VMEM((h3, QUERIES, 256), F32),
-            pltpu.VMEM((h3, 4, BLOCK, 128), BF16),
-            pltpu.VMEM((h3, 4, BLOCK, 128), BF16),
-            pltpu.VMEM((h3, 4, 8, BLOCK), F32),
-            pltpu.VMEM((h3, 4, 8, BLOCK), F32),
+            pltpu.VMEM((h3, 2, BLOCK, 128), BF16),
+            pltpu.VMEM((h3, 2, BLOCK, 128), BF16),
+            pltpu.VMEM((h3, 2, 8, BLOCK), F32),
+            pltpu.VMEM((h3, 2, 8, BLOCK), F32),
+            pltpu.VMEM((h3, BLOCK, 128), BF16),
+            pltpu.VMEM((h3, BLOCK, 128), BF16),
+            pltpu.VMEM((h3, 8, BLOCK), F32),
+            pltpu.VMEM((h3, 8, BLOCK), F32),
             pltpu.VMEM((h3, BLOCK, 128), BF16),
             pltpu.VMEM((CHUNKS, 8, ROWS, CHUNK), BF16),
             pltpu.VMEM((CHUNKS, 7, ROWS, CHUNK), BF16),
@@ -580,7 +617,7 @@
             dma((8,)), dma((PARTS, 7)), dma((PARTS, 7)), dma((4, 8)), dma((4, 8)), dma((2, 8)),
             dma((h3, 4)), dma((h3, 4)),
             dma((PARTS, h3, 4)), dma((PARTS, h3, 4)), dma((PARTS, h3, 4)), dma((PARTS, h3, 4)),
-            dma((h3, 4)), dma((h3, 4)), dma((h3, 4)), dma((h3, 4)),
+            dma((h3, 4)), dma((h3, 4)),
             dma((CHUNKS, 7)), dma((CHUNKS, 7)),
         ],
         compiler_params=pltpu.CompilerParams(

time: 91.8 us -> 88 us (0.959)
  Pallas kernels: 90.1 us -> 86.3 us
    pallas_call x1, Pallas kernels: 90.1 us -> 86.3 us  [per_device(): pl.pallas_call(kernel, out_shape=jax.ShapeDtypeStruct((ROWS, D), BF16), i...]
where the time goes in v3:
time: 88 us; the launch traced here: 87.9 us
  Pallas kernels  86.3 us (98%)
  local copies, waits for them, and re-layouts  1.62 us (2%)
    pallas_call x1, Pallas kernels, per_device(): pl.pallas_call(kernel, out_shape=jax.ShapeDtypeStruct((ROWS, D), BF16), i...  86.3 us

profile of v3, /device:TPU:1, one launch (start us, length us, event | category | flops | bytes accessed | tf_op | source)
XLA Modules:
  0.0 87.9 jit_solution(904178516074955030)
XLA Ops:
  0.0 86.3 %joint_attention.1 = bf16[32,3072]{1,0:T(8,128)(2,1)} custom-call(bf16[32,3072]{1,0:T(8,128)(2,1)} %img_hbm.1, bf16[8,3072]{1,0:T(8,128)(2,1)} %text_hbm.1, f32[3,3072]{1,0:T(4,128)} %mod_hbm.1, f32[2,3072]{1,0:T(2,128)} %tmod_hbm.1, f32[3,128]{1,0:T(4,128)} %gains_hbm.1, bf16[3,3072,384]{2,1,0:T(8,128)(2,1)} %bitcast.2, bf16[3,96,256]{2,1,0:T(8,128)(2,1)} %bitcast.3, ...), custom_call_target="tpu_custom_call" | custom-call | tf_op jit(solution)/shard_map/joint_attention/pallas_call | solution.py:575
  86.3 1.6 %copy.10 = bf16[32,3072]{1,0:T(8,128)(2,1)} copy(bf16[32,3072]{1,0:T(8,128)(2,1)} %joint_attention.1) | data formatting | bytes 393216

commit v4 on v3

--- a/solution.py
+++ b/solution.py
@@ -113,6 +113,49 @@
     for k in range(PARTS):
         tok[k, 0] = normed[k * PART : (k + 1) * PART]
 
+    pl.semaphore_wait(barrier, 14)
+
+    quad = c * 2 + xl
+
+    def a1_copy(j):
+        to = lax.rem(c + j % 2, 2) * 2 + lax.rem(xl + j // 2, 2)
+        return pltpu.make_async_remote_copy(
+            src_ref=a1_send.at[to], dst_ref=a1_recv.at[quad],
+            send_sem=a_sems.at[0, j], recv_sem=a_sems.at[1, j],
+            device_id=quad_peer(j), device_id_type=MESH,
+        )
+
+    def a2_copy(dz):
+        return pltpu.make_async_remote_copy(
+            src_ref=a2_send.at[lax.rem(z + dz, 8)], dst_ref=a2_recv.at[z],
+            send_sem=a_sems.at[2, dz], recv_sem=a_sems.at[3, dz],
+            device_id=line_peer(dz), device_id_type=MESH,
+        )
+
+    def token_copy(k, i):
+        source, (dy, dx) = TOKEN_HOPS[i]
+        return pltpu.make_async_remote_copy(
+            src_ref=tok.at[k, source], dst_ref=tok.at[k, i + 1],
+            send_sem=tok_send.at[k, i], recv_sem=tok_recv.at[k, i],
+            device_id={"ulysses": ulysses_peer(dy, dx)}, device_id_type=MESH,
+        )
+
+    def token_near(k):
+        for i in (3, 0, 1):
+            token_copy(k, i).start()
+
+    def token_onward(k):
+        for source, onward in ((0, 4), (1, 5), (3, 6)):
+            token_copy(k, source).wait_recv()
+            token_copy(k, onward).start()
+        token_copy(k, 2).start()
+
+    def token_rest(k):
+        for i in (2, 4, 5, 6):
+            token_copy(k, i).wait_recv()
+
+    token_near(0)
+
     for load in small[2:]:
         load.wait()
     cap = layer_norm(text_ref[...].astype(F32), tmod_ref[0:1, :], tmod_ref[1:2, :]).astype(F32)
@@ -133,51 +176,8 @@
             a1_send[c_ * 2 + xl_] = rows.astype(BF16)
     for h in range(HEADS_HERE):
         w_cap[h, CAP_COLS:128, :] = jnp.zeros((128 - CAP_COLS, 256), BF16)
-
-    pl.semaphore_wait(barrier, 14)
-
-    quad = c * 2 + xl
-
-    def a1_copy(j):
-        to = lax.rem(c + j % 2, 2) * 2 + lax.rem(xl + j // 2, 2)
-        return pltpu.make_async_remote_copy(
-            src_ref=a1_send.at[to], dst_ref=a1_recv.at[quad],
-            send_sem=a_sems.at[0, j], recv_sem=a_sems.at[1, j],
-            device_id=quad_peer(j), device_id_type=MESH,
-        )
-
-    def a2_copy(dz):
-        return pltpu.make_async_remote_copy(
-            src_ref=a2_send.at[lax.rem(z + dz, 8)], dst_ref=a2_recv.at[z],
-            send_sem=a_sems.at[2, dz], recv_sem=a_sems.at[3, dz],
-            device_id=line_peer(dz), device_id_type=MESH,
-        )
-
-    def token_copy(k, i):
-        source, (dy, dx) = TOKEN_HOPS[i]
-        return pltpu.make_async_remote_copy(
-            src_ref=tok.at[k, source], dst_ref=tok.at[k, i + 1],
-            send_sem=tok_send.at[k, i], recv_sem=tok_recv.at[k, i],
-            device_id={"ulysses": ulysses_peer(dy, dx)}, device_id_type=MESH,
-        )
-
-    def token_near(k):
-        for i in (3, 0, 1):
-            token_copy(k, i).start()
-
-    def token_onward(k):
-        for source, onward in ((0, 4), (1, 5), (3, 6)):
-            token_copy(k, source).wait_recv()
-            token_copy(k, onward).start()
-        token_copy(k, 2).start()
-
-    def token_rest(k):
-        for i in (2, 4, 5, 6):
-            token_copy(k, i).wait_recv()
-
     for j in range(1, 4):
         a1_copy(j).start()
-    token_near(0)
 
     other_c, other_xl = lax.rem(c + 1, 2), lax.rem(xl + 1, 2)
     r1_copy = pltpu.make_async_remote_copy(
@@ -225,10 +225,18 @@
 
     def query_copy(h, j):
         return pltpu.make_async_remote_copy(
-            src_ref=q_buf.at[h, 0], dst_ref=q_buf.at[h, j],
+            src_ref=q_buf.at[h, 2 if j == 3 else 0], dst_ref=q_buf.at[h, j],
             send_sem=q_send.at[h, j], recv_sem=q_recv.at[h, j],
-            device_id=quad_peer(j), device_id_type=MESH,
-        )
+            device_id=quad_peer(2 if j == 2 else 1), device_id_type=MESH,
+        )
+
+    def query_onward():
+        def head(h, carry):
+            query_copy(h, 2).wait_recv()
+            query_copy(h, 3).start()
+            return carry
+
+        lax.fori_loop(0, HEADS_HERE, head, 0)
 
     def forward(k, h, s):
         ring_right(k, h, s - 1).wait_recv()
@@ -246,7 +254,7 @@
             ring_left(k, h, 1).start()
             q_buf[h, 0, k] = root_norm(projected[:, 0:128], gains_ref[0:1, :] * QUERY_SCALE)
             if k == PARTS - 1:
-                for j in range(1, 4):
+                for j in (2, 1):
                     query_copy(h, j).start()
             return carry
 
@@ -363,13 +371,15 @@
     project(1)
     cap_line()
     forward_all(1, 2)
+    query_onward()
     forward_all(0, 3)
 
     def step_three(h, carry):
         forward(1, h, 3)
-        for j in range(1, 4):
+        for j in (1, 3):
             query_copy(h, j).wait_recv()
-        attend(h, [0, 1, 7], first=True)
+        attend(h, [0, 1], first=True)
+        attend(h, [7, 2])
         return carry
 
     lax.fori_loop(0, HEADS_HERE, step_three, 0)
@@ -384,8 +394,8 @@
         cap_kv = cap_all[:, :, col].astype(F32)
         cap_keys = cap_kv[:, 0:8, :].reshape(64, 128).astype(BF16)
         cap_values = cap_kv[:, 8:16, :].reshape(64, 128).astype(BF16)
-        attend(h, [2, 6], caption=(cap_keys, cap_values))
-        attend(h, [3, 5])
+        attend(h, [6, 3])
+        attend(h, [5], caption=(cap_keys, cap_values))
         return carry
 
     lax.fori_loop(0, HEADS_HERE, step_four, 0)
@@ -460,11 +470,17 @@
         x_copy(h).start()
         x_level_copy(h).start()
 
-    for h in range(HEADS_HERE):
+    def last_loop(h, carry):
         step_last(h)
-        if h > 0:
-            step_pair(h - 1)
-    step_pair(HEADS_HERE - 1)
+        return carry
+
+    lax.fori_loop(0, HEADS_HERE, last_loop, 0)
+
+    def pair_loop(h, carry):
+        step_pair(h)
+        return carry
+
+    lax.fori_loop(0, HEADS_HERE, pair_loop, 0)
 
     def combine(h, carry):
         x_copy(h).wait_recv()

time: 88 us -> 86.5 us (0.983)
  Pallas kernels: 86.3 us -> 84.8 us
    pallas_call x1, Pallas kernels: 86.3 us -> 84.8 us  [per_device(): pl.pallas_call(kernel, out_shape=jax.ShapeDtypeStruct((ROWS, D), BF16), i...]
where the time goes in v4:
time: 86.5 us; the launch traced here: 86.4 us
  Pallas kernels  84.8 us (98%)
  local copies, waits for them, and re-layouts  1.62 us (2%)
    pallas_call x1, Pallas kernels, per_device(): pl.pallas_call(kernel, out_shape=jax.ShapeDtypeStruct((ROWS, D), BF16), i...  84.8 us

profile of v4, /device:TPU:1, one launch (start us, length us, event | category | flops | bytes accessed | tf_op | source)
XLA Modules:
  0.0 86.4 jit_solution(16253482738373751021)
XLA Ops:
  0.0 84.8 %joint_attention.1 = bf16[32,3072]{1,0:T(8,128)(2,1)} custom-call(bf16[32,3072]{1,0:T(8,128)(2,1)} %img_hbm.1, bf16[8,3072]{1,0:T(8,128)(2,1)} %text_hbm.1, f32[3,3072]{1,0:T(4,128)} %mod_hbm.1, f32[2,3072]{1,0:T(2,128)} %tmod_hbm.1, f32[3,128]{1,0:T(4,128)} %gains_hbm.1, bf16[3,3072,384]{2,1,0:T(8,128)(2,1)} %bitcast.2, bf16[3,96,256]{2,1,0:T(8,128)(2,1)} %bitcast.3, ...), custom_call_target="tpu_custom_call" | custom-call | tf_op jit(solution)/shard_map/joint_attention/pallas_call | solution.py:591
  84.8 1.6 %copy.10 = bf16[32,3072]{1,0:T(8,128)(2,1)} copy(bf16[32,3072]{1,0:T(8,128)(2,1)} %joint_attention.1) | data formatting | bytes 393216

commit v5 on v4

--- a/solution.py
+++ b/solution.py
@@ -75,6 +75,17 @@
     def line_peer(dz):
         return {"blk": blk_of(xl, lax.rem(z + dz, 8), c)}
 
+    barrier = pltpu.get_barrier_semaphore()
+    for dy, dx in NEAR_STEPS:
+        pl.semaphore_signal(
+            barrier, inc=1, device_id={"ulysses": ulysses_peer(dy, dx)}, device_id_type=MESH
+        )
+
+    for j in range(1, 4):
+        pl.semaphore_signal(barrier, inc=1, device_id=quad_peer(j), device_id_type=MESH)
+    for dz in range(1, 8):
+        pl.semaphore_signal(barrier, inc=1, device_id=line_peer(dz), device_id_type=MESH)
+
     load_cap = pltpu.make_async_copy(tkv_hbm, w_cap.at[:, pl.ds(0, CAP_COLS), :], w_sem.at[0])
     load_qkv = pltpu.make_async_copy(qkv_hbm, w_qkv, w_sem.at[1])
     load_out = pltpu.make_async_copy(out_hbm, w_out, w_sem.at[2])
@@ -96,17 +107,6 @@
     load_qkv.start()
     load_out.start()
 
-    barrier = pltpu.get_barrier_semaphore()
-    for dy, dx in NEAR_STEPS:
-        pl.semaphore_signal(
-            barrier, inc=1, device_id={"ulysses": ulysses_peer(dy, dx)}, device_id_type=MESH
-        )
-
-    for j in range(1, 4):
-        pl.semaphore_signal(barrier, inc=1, device_id=quad_peer(j), device_id_type=MESH)
-    for dz in range(1, 8):
-        pl.semaphore_signal(barrier, inc=1, device_id=line_peer(dz), device_id_type=MESH)
-
     small[0].wait()
     small[1].wait()
     normed = layer_norm(img_ref[...].astype(F32), mod_ref[0:1, :], mod_ref[1:2, :])
@@ -145,10 +145,12 @@
             token_copy(k, i).start()
 
     def token_onward(k):
-        for source, onward in ((0, 4), (1, 5), (3, 6)):
+        for source, onward in ((0, 4), (1, 5)):
             token_copy(k, source).wait_recv()
             token_copy(k, onward).start()
         token_copy(k, 2).start()
+        token_copy(k, 3).wait_recv()
+        token_copy(k, 6).start()
 
     def token_rest(k):
         for i in (2, 4, 5, 6):

time: 86.5 us -> 86.4 us (level)
  no operation moved by 1% of the time
where the time goes in v5:
time: 86.4 us; the launch traced here: 86.3 us
  Pallas kernels  84.7 us (98%)
  local copies, waits for them, and re-layouts  1.62 us (2%)
    pallas_call x1, Pallas kernels, per_device(): pl.pallas_call(kernel, out_shape=jax.ShapeDtypeStruct((ROWS, D), BF16), i...  84.7 us

profile of v5, /device:TPU:1, one launch (start us, length us, event | category | flops | bytes accessed | tf_op | source)
XLA Modules:
  0.0 86.3 jit_solution(1943602431511250713)
XLA Ops:
  0.0 84.7 %joint_attention.1 = bf16[32,3072]{1,0:T(8,128)(2,1)} custom-call(bf16[32,3072]{1,0:T(8,128)(2,1)} %img_hbm.1, bf16[8,3072]{1,0:T(8,128)(2,1)} %text_hbm.1, f32[3,3072]{1,0:T(4,128)} %mod_hbm.1, f32[2,3072]{1,0:T(2,128)} %tmod_hbm.1, f32[3,128]{1,0:T(4,128)} %gains_hbm.1, bf16[3,3072,384]{2,1,0:T(8,128)(2,1)} %bitcast.2, bf16[3,96,256]{2,1,0:T(8,128)(2,1)} %bitcast.3, ...), custom_call_target="tpu_custom_call" | custom-call | tf_op jit(solution)/shard_map/joint_attention/pallas_call | solution.py:593
  84.7 1.6 %copy.10 = bf16[32,3072]{1,0:T(8,128)(2,1)} copy(bf16[32,3072]{1,0:T(8,128)(2,1)} %joint_attention.1) | data formatting | bytes 393216
